TPU v7x, 128 devices: a whole 4x4x4 slice. The times are simulated.
128 devices in a mesh: dp: 16 (over y, x), seq: 8 (over z, core).
Axes of the slice: x: 4, y: 4, z: 4, core: 2. Of those that a mesh axis runs over, the one named last changes fastest.
Arguments:
- queries: bfloat16 [16, 1024, 4096], P('dp', 'seq'), may hold values from -8 to 8
- grad_out: bfloat16 [16, 1024, 4096], P('dp', 'seq'), may hold values from -6 to 6
- kv_store: bfloat16 [16, 8, 640, 1024], P('dp', None, 'seq'), may hold values from -6 to 6
- tile_owner: int32 [16, 8], replicated, may hold values from 0 to 15, as said below
- tile_counts: int32 [16, 3], replicated, may hold values from 1 to 4, 8 in all within a row
- span_image: int32 [16, 8], replicated, may hold values from 0 to 2
Outputs:
- attn_out: bfloat16 [16, 1024, 4096], P('dp', 'seq')
- grad_q: bfloat16 [16, 1024, 4096], P('dp', 'seq')
- grad_kv: bfloat16 [16, 8, 640, 1024], P('dp', None, 'seq')
Inputs may be any that keep to these rules, and one draw needn't show every extreme that they name: tile_owner[g, j] = (g + c_j) mod 16, one offset c_j for each slot j, the 8 offsets all different. `tile_counts`: the counts of one sample sum to 8.
All inputs are finite; a program needn't handle non-finite values.
Results may differ from a plain program's by a relative error of at most 0.012.
Values may be sent and summed in bfloat16 or wider, within the bound.
No kernel may reach another device: no remote copies, remote signals or barrier semaphores. Data moves between devices by JAX's collectives and lax.ppermute only.
A program may use at most 128 MiB of HBM per device.

v0:
```python
import jax
import jax.numpy as jnp
from jax import lax
from jax.experimental import pallas as pl
from jax.experimental.pallas import tpu as pltpu
from jax.sharding import PartitionSpec as P

HD = 128
HQ = 32
KVH = 4
GROUP = 8
TT = 640
TPS = 8
IMGS = 3
MAXT = 4
TOK = 128
N_SEQ = 8
CHIPS = 4
ROWS = TT // N_SEQ
KW = KVH * HD
QW = GROUP * HD
LINES = GROUP * TOK
SCALE = HD**-0.5
PIECE = (TPS, ROWS, HD)
PIECES = (TPS, CHIPS, ROWS, HD)
EXP_SCALE = SCALE * 1.4426950408889634
BF = jnp.bfloat16
F32 = jnp.float32


def run_copies(pairs):
    for (source, where), (target, there) in pairs:
        target[there] = source[where]


def whole(shape):
    zeros = (0,) * len(shape)
    return pl.BlockSpec(shape, lambda i, t: zeros)


def copier(body, shapes, table, *arrays, after=()):
    return pl.pallas_call(
        body,
        out_shape=shapes,
        grid_spec=pltpu.PrefetchScalarGridSpec(
            num_scalar_prefetch=1,
            grid=(1,),
            in_specs=[whole(a.shape) for a in arrays]
            + [pl.BlockSpec(memory_space=pl.ANY)] * len(after),
            out_specs=jax.tree.map(lambda a: whole(a.shape), shapes),
        ),
        compiler_params=pltpu.CompilerParams(vmem_limit_bytes=32 * 2**20),
    )(table, *arrays, *after)


def struct(*shape):
    return jax.ShapeDtypeStruct(shape, BF)


def column(index, width):
    return pl.ds(pl.multiple_of(index * width, width), width)


def outgoing_heads(peers, store, part, *text):
    def body(t, s, *rest):
        outs = rest[len(text) :]
        for k in range(CHIPS):
            outs[k][...] = s[:, :, column(t[k], HD)]
        for i in range(len(text)):
            for k in range(1, CHIPS):
                outs[CHIPS + 3 * i + k - 1][...] = rest[i][:, column(t[k], QW)]

    shapes = (struct(*PIECE),) * CHIPS + (struct(TOK, QW),) * (3 * len(text))
    return pl.pallas_call(
        body,
        out_shape=shapes,
        grid_spec=pltpu.PrefetchScalarGridSpec(
            num_scalar_prefetch=1,
            grid=(1,),
            in_specs=[pl.BlockSpec((TPS, ROWS, KW), lambda i, t: (0, 0, part))]
            + [whole(x.shape) for x in text],
            out_specs=jax.tree.map(lambda a: whole(a.shape), shapes),
        ),
        compiler_params=pltpu.CompilerParams(vmem_limit_bytes=32 * 2**20),
    )(peers, store, *text)


def fence(x, *after):
    def body(*refs):
        pass

    return pl.pallas_call(
        body,
        out_shape=jax.ShapeDtypeStruct(x.shape, x.dtype),
        in_specs=[pl.BlockSpec(memory_space=pl.ANY)] * (1 + len(after)),
        out_specs=pl.BlockSpec(memory_space=pl.ANY),
        input_output_aliases={0: 0},
    )(x, *after)


def outgoing_pieces(group_of, pieces, *after):
    def body(t, *rest):
        for j in range(TPS):
            for k in range(CHIPS):
                rest[-1][t[j], k] = rest[k][j]

    return copier(body, struct(16, *PIECES[1:]), group_of, *pieces, after=after)


def chosen(table, arrived, *after):
    def body(t, s, *rest):
        for j in range(TPS):
            rest[-1][j] = s[t[j]]

    return copier(body, struct(*PIECES), table, arrived, after=after)


def outgoing_sums(owner, own, other):
    def body(t, a, b, *rest):
        for j in range(TPS):
            rest[-1][t[j]] = (a[j] + b[j].astype(F32)).astype(BF)

    return copier(body, struct(16, *PIECES[1:]), owner, own, other)


def chosen_pieces(group_of, arrived):
    def body(t, s, *outs):
        for j in range(TPS):
            for k in range(CHIPS):
                outs[k][j] = s[t[j], k]

    return copier(body, (struct(*PIECE),) * CHIPS, group_of, arrived)


def stored_tiles(peers, keys, values):
    def body(t, *rest):
        for part in range(2):
            for k in range(CHIPS):
                where = column(t[k] + part * KVH, HD)
                rest[-1][:, :, where] = rest[part * CHIPS + k][...]

    return copier(body, struct(TPS, ROWS, 2 * KW), peers, *keys, *values)


def text_rows(peers, chunks):
    def body(t, *rest):
        for k in range(CHIPS):
            rest[CHIPS][:, column(t[k], QW)] = rest[k][...]

    return copier(body, struct(TOK, HQ * HD), peers, *chunks)


LANES = [slice(i * HD, (i + 1) * HD) for i in range(TT // HD)]
HEADS = [slice(h * TOK, (h + 1) * TOK) for h in range(GROUP)]
CH_S, CH_O, CH_D = 256, 512, 512


def cuts(size):
    return [slice(i, i + size) for i in range(0, LINES, size)]


def wide(column, rows):
    return jnp.broadcast_to(column, (rows, HD))


def fill_tiles(core, target, mine, other):
    for k in range(CHIPS):
        here = pl.multiple_of(core * (TT // 2) + k * ROWS, 16)
        there = pl.multiple_of((1 - core) * (TT // 2) + k * ROWS, 16)

        @pl.loop(0, TPS)
        def _(j):
            target[j, pl.ds(here, ROWS), :] = mine[j, k]
            target[j, pl.ds(there, ROWS), :] = other[j, k]


def split_tiles(core, total, scale, mine, other):
    @pl.loop(0, TPS)
    def _(j):
        rows = (total[j] * scale).T
        halves = [rows[: TT // 2].reshape(CHIPS, ROWS, HD), rows[TT // 2 :].reshape(CHIPS, ROWS, HD)]
        for p in range(2):

            @pl.when(core == p)
            def _():
                mine[j] = halves[p]
                other[j] = halves[1 - p].astype(BF)


def load_text(b, target, chunks):
    for k, chunk in enumerate(chunks):

        @pl.when(b == k)
        def _():
            for h, rows in enumerate(HEADS):
                target[rows, :] = chunk[:, h * HD : (h + 1) * HD]


def store_text(b, chunks, value):
    for k, chunk in enumerate(chunks):

        @pl.when(b == k)
        def _():
            for h, rows in enumerate(HEADS):
                chunk[:, h * HD : (h + 1) * HD] = value(rows)


def weights_body(
    info, q0, q1, q2, q3, k_mine, k_other, e_out, w_out, k_s, kt_s, q_s, m_s, l_s, top_s, sum_s
):
    b = pl.program_id(0)
    first, number = info[0, b], info[1, b]

    @pl.when(b == 0)
    def _():
        fill_tiles(info[2, 1], k_s, k_mine, k_other)

        @pl.loop(0, TPS)
        def _(j):
            kt_s[j] = k_s[j].T

    load_text(b, q_s, (q0, q1, q2, q3))
    top_s[...] = jnp.full(top_s.shape, -jnp.inf, F32)
    sum_s[...] = jnp.zeros_like(sum_s)
    w_out[...] = jnp.zeros_like(w_out)

    @pl.loop(0, number)
    def _(t):
        j = first + t
        for rows in cuts(CH_S):
            s = jnp.dot(q_s[rows, :], kt_s[j], preferred_element_type=F32)
            top = s[:, LANES[0]]
            for part in LANES[1:]:
                top = jnp.maximum(top, s[:, part])
            top = wide(jnp.max(top, axis=1, keepdims=True), CH_S)
            m_s[t, rows, :] = top
            top_s[rows, :] = jnp.maximum(top_s[rows, :], top)
            top = top * EXP_SCALE
            total = None
            for part in LANES:
                e = jnp.exp2(s[:, part] * EXP_SCALE - top)
                e_out[0, t, rows, part] = e.astype(BF)
                total = e if total is None else total + e
            l_s[t, rows, :] = total

    @pl.loop(0, number)
    def _(t):
        f = jnp.exp2((m_s[t] - top_s[...]) * EXP_SCALE)
        m_s[t] = f
        sum_s[...] += f * l_s[t]

    for rows in HEADS:
        total = jnp.sum(sum_s[rows, :], axis=1, keepdims=True)
        sum_s[rows, :] = wide(1.0 / total, TOK)

    @pl.loop(0, number)
    def _(t):
        lane = lax.broadcasted_iota(jnp.int32, W_SHAPE, 1)
        w_out[0] = jnp.where(lane == t, m_s[t] * sum_s[...], w_out[0])


def outputs_body(
    info, g0, g1, g2, g3, e, w, v_mine, v_other, o0, o1, o2, o3, d_out, mine, other,
    v_s, dvt_s, d_s, acc_s,
):
    b = pl.program_id(0)
    core = info[2, 1]
    first, number = info[0, b], info[1, b]

    @pl.when(b == 0)
    def _():
        fill_tiles(core, v_s, v_mine, v_other)

        @pl.loop(0, TPS)
        def _(j):
            dvt_s[j] = jnp.zeros((HD, TT), F32)

    load_text(b, d_s, (g0, g1, g2, g3))
    acc_s[...] = jnp.zeros_like(acc_s)

    @pl.loop(0, number)
    def _(t):
        j = first + t
        lane = lax.broadcasted_iota(jnp.int32, (CH_O, HD), 1)
        for rows in cuts(CH_O):
            weight = jnp.sum(jnp.where(lane == t, w[0, rows, :], 0.0), axis=1, keepdims=True)
            acc_s[rows, :] += weight * jnp.dot(e[0, t, rows, :], v_s[j], preferred_element_type=F32)
            d_out[0, t, rows, :] = (d_s[rows, :].astype(F32) * weight).astype(BF)
        dvt_s[j] += jnp.dot(d_out[0, t].T, e[0, t], preferred_element_type=F32)

    store_text(b, (o0, o1, o2, o3), lambda rows: acc_s[rows, :].astype(BF))

    @pl.when(b == CHIPS - 1)
    def _():
        split_tiles(core, dvt_s, 1.0, mine, other)


def grads_body(
    info, q0, q1, q2, q3, e, d, a0, a1, a2, a3, k_mine, k_other, v_mine, v_other,
    o0, o1, o2, o3, mine, other,
    k_s, vt_s, dkt_s, q_s, acc_s, a_s, ds_s,
):
    b = pl.program_id(0)
    core = info[2, 1]
    first, number = info[0, b], info[1, b]

    @pl.when(b == 0)
    def _():
        fill_tiles(core, k_s, v_mine, v_other)

        @pl.loop(0, TPS)
        def _(j):
            vt_s[j] = k_s[j].T
            dkt_s[j] = jnp.zeros((HD, TT), F32)

        fill_tiles(core, k_s, k_mine, k_other)

    load_text(b, q_s, (q0, q1, q2, q3))
    load_text(b, a_s, (a0, a1, a2, a3))
    acc_s[...] = jnp.zeros_like(acc_s)

    @pl.loop(0, number)
    def _(t):
        j = first + t
        for rows in cuts(CH_D):
            dp = jnp.dot(d[0, t, rows, :], vt_s[j], preferred_element_type=F32)
            dot = jnp.sum(
                d[0, t, rows, :].astype(F32) * a_s[rows, :].astype(F32), axis=1, keepdims=True
            )
            ds = (e[0, t, rows, :].astype(F32) * (dp - dot)).astype(BF)
            ds_s[rows, :] = ds
            acc_s[rows, :] += jnp.dot(ds, k_s[j], preferred_element_type=F32)
        dkt_s[j] += jnp.dot(q_s[...].T, ds_s[...], preferred_element_type=F32)

    store_text(b, (o0, o1, o2, o3), lambda rows: (acc_s[rows, :] * SCALE).astype(BF))

    @pl.when(b == CHIPS - 1)
    def _():
        split_tiles(core, dkt_s, SCALE, mine, other)


def fixed(shape):
    zeros = (0,) * len(shape)
    return pl.BlockSpec(shape, lambda b, t: zeros, pipeline_mode=pl.Buffered(1))


def kept(shape):
    zeros = (0,) * len(shape)
    return pl.BlockSpec(shape, lambda b, t: zeros)


def by_block(*shape):
    zeros = (0,) * len(shape)
    return pl.BlockSpec((1,) + shape, lambda b, t: (b,) + zeros)


OWN_TEXT = pl.BlockSpec((TOK, QW), lambda b, t: (0, t[2, 0]), pipeline_mode=pl.Buffered(1))
E_SHAPE = (MAXT, LINES, TT)
D_SHAPE = (MAXT, LINES, HD)
W_SHAPE = (LINES, HD)


def attention_call(body, matmuls, out_shape, in_specs, out_specs, scratch_shapes):
    return pl.pallas_call(
        body,
        out_shape=out_shape,
        grid_spec=pltpu.PrefetchScalarGridSpec(
            num_scalar_prefetch=1,
            grid=(CHIPS,),
            in_specs=in_specs,
            out_specs=out_specs,
            scratch_shapes=scratch_shapes,
        ),
        compiler_params=pltpu.CompilerParams(vmem_limit_bytes=56 * 2**20),
        cost_estimate=pl.CostEstimate(
            flops=20 * matmuls * LINES * CHIPS * 3 * TT * HD,
            bytes_accessed=30 * 2**20,
            transcendentals=0,
        ),
    )


TEXT = [OWN_TEXT] + [fixed((TOK, QW))] * 3
TEXT_OUT = (struct(TOK, QW),) * 4
TEXT_KEPT = (kept((TOK, QW)),) * 4
TILES = [fixed(PIECES)] * 2
TILES_OUT = (jax.ShapeDtypeStruct(PIECES, F32), struct(*PIECES))
TILES_KEPT = (kept(PIECES),) * 2
TILE_ROWS, TILE_COLUMNS = (TPS, TT, HD), (TPS, HD, TT)


def weights(info, queries, tiles):
    return attention_call(
        weights_body,
        2,
        (struct(CHIPS, *E_SHAPE), jax.ShapeDtypeStruct((CHIPS,) + W_SHAPE, F32)),
        TEXT + TILES,
        (by_block(*E_SHAPE), by_block(*W_SHAPE)),
        [
            pltpu.VMEM(TILE_ROWS, BF),
            pltpu.VMEM(TILE_COLUMNS, BF),
            pltpu.VMEM((LINES, HD), BF),
            pltpu.VMEM((MAXT, LINES, HD), F32),
            pltpu.VMEM((MAXT, LINES, HD), F32),
            pltpu.VMEM((LINES, HD), F32),
            pltpu.VMEM((LINES, HD), F32),
        ],
    )(info, *queries, *tiles)


def outputs(info, grads, e, w, tiles):
    return attention_call(
        outputs_body,
        2,
        TEXT_OUT + (struct(CHIPS, *D_SHAPE),) + TILES_OUT,
        TEXT + [by_block(*E_SHAPE), by_block(*W_SHAPE)] + TILES,
        TEXT_KEPT + (by_block(*D_SHAPE),) + TILES_KEPT,
        [
            pltpu.VMEM(TILE_ROWS, BF),
            pltpu.VMEM(TILE_COLUMNS, F32),
            pltpu.VMEM((LINES, HD), BF),
            pltpu.VMEM((LINES, HD), F32),
        ],
    )(info, *grads, e, w, *tiles)


def gradients(info, queries, e, d, attn, keys, values):
    return attention_call(
        grads_body,
        3,
        TEXT_OUT + TILES_OUT,
        TEXT
        + [by_block(*E_SHAPE), by_block(*D_SHAPE)]
        + [fixed((TOK, QW))] * 4
        + TILES * 2,
        TEXT_KEPT + TILES_KEPT,
        [
            pltpu.VMEM(TILE_ROWS, BF),
            pltpu.VMEM(TILE_COLUMNS, BF),
            pltpu.VMEM(TILE_COLUMNS, F32),
            pltpu.VMEM((LINES, HD), BF),
            pltpu.VMEM((LINES, HD), F32),
            pltpu.VMEM((LINES, HD), BF),
            pltpu.VMEM((LINES, TT), BF),
        ],
    )(info, *queries, e, d, *attn, *keys, *values)


def swap(x, mask):
    return lax.ppermute(x, "seq", [(i, i ^ mask) for i in range(N_SEQ)])


def spread(chunks):
    return [chunks[0]] + [swap(chunks[k], 2 * k) for k in range(1, CHIPS)]


def shards(queries, grad_out, kv_store, tile_owner, tile_counts, span_image):
    my_group = lax.axis_index("dp")
    my_seq = lax.axis_index("seq")
    chip, core = my_seq // 2, my_seq % 2
    queries, grad_out, store = queries[0], grad_out[0], kv_store[0]

    groups = jnp.arange(tile_owner.shape[0], dtype=jnp.int32)
    group_of = jnp.sum(jnp.where(tile_owner == my_group, groups[:, None], 0), axis=0).astype(
        jnp.int32
    )
    owner = lax.dynamic_index_in_dim(tile_owner, my_group, 0, keepdims=False)
    peers = (chip ^ jnp.arange(CHIPS, dtype=jnp.int32)).astype(jnp.int32)
    counts = lax.dynamic_index_in_dim(tile_counts, my_group, 0, keepdims=False)
    starts = jnp.cumsum(counts) - counts
    images = lax.dynamic_index_in_dim(span_image, my_group, 0, keepdims=False)
    blocks = peers * 2 + core
    mine = jnp.sum(
        jnp.where(blocks[:, None] == jnp.arange(N_SEQ)[None, :], images[None, :], 0), axis=1
    )
    pick = mine[:, None] == jnp.arange(IMGS, dtype=jnp.int32)[None, :]
    first = jnp.sum(jnp.where(pick, starts[None, :], 0), axis=1)
    number = jnp.sum(jnp.where(pick, counts[None, :], 0), axis=1)
    place = jnp.stack([chip, core, chip, core])
    info = jnp.stack([first, number, place]).astype(jnp.int32)

    def exchange(x):
        return lax.all_to_all(x, "dp", split_axis=0, concat_axis=0, tiled=True)

    k_pieces = outgoing_heads(peers, store, 0)
    pieces = outgoing_heads(peers, store, 1, queries, grad_out)
    v_pieces, texts = pieces[:CHIPS], pieces[CHIPS:]
    q_text = spread([queries, *texts[:3]])
    g_text = spread([grad_out, *texts[3:]])
    keys = exchange(outgoing_pieces(group_of, spread(k_pieces), v_pieces[0]))
    values = outgoing_pieces(group_of, spread(v_pieces), info, *q_text[1:])
    keys = chosen(owner, keys, values)
    keys = keys, swap(keys, 1)
    e, w = weights(info, q_text, keys)
    values = chosen(owner, exchange(values), w, *g_text[1:])
    values = values, swap(values, 1)

    *attn, d, dv_mine, dv_other = outputs(info, g_text, e, w, values)
    attn_text = spread(attn)
    *grad_q, dk_mine, dk_other = gradients(info, q_text, e, d, attn, keys, values)
    dk_other = fence(dk_other, *attn_text[1:])

    def scatter(own, other):
        arrived = exchange(outgoing_sums(owner, own, swap(other, 1)))
        return spread(chosen_pieces(group_of, arrived))

    dv = scatter(dv_mine, dv_other)
    dk = scatter(dk_mine, dk_other)
    grad_kv = stored_tiles(peers, dk, dv)
    attn_rows = text_rows(peers, attn_text)
    grad_rows = text_rows(peers, spread(grad_q))
    return (attn_rows[None], grad_rows[None], grad_kv[None])


def solution(mesh):
    placed = (P("dp", "seq", None), P("dp", "seq", None), P("dp", None, "seq", None), P(), P(), P())
    return jax.shard_map(
        shards,
        mesh=mesh,
        in_specs=placed,
        out_specs=(P("dp", "seq", None), P("dp", "seq", None), P("dp", None, "seq", None)),
        check_vma=False,
    )
```

profile of v0, /device:TPU:0, one launch (start us, length us, event | category | flops | bytes accessed | tf_op | source)
XLA Modules:
  0.0 206.6 jit_solution(4972333729062895429)
XLA Ops:
  1.2 1.3 copy-done.1
  2.5 1.4 shard_map.86
  3.9 2.0 collective-permute-start.6
  5.9 3.6 %collective-permute-start.7 = (bf16[8,80,128]{2,1,0:T(8,128)(2,1)S(1)}, bf16[8,80,128]{2,1,0:T(8,128)(2,1)S(1)}, u32[]{:S(2)}, u32[]{:S(2)}) collective-permute-start(bf16[8,80,128]{2,1,0:T(8,128)(2,1)S(1)} %get-tuple-element.48), channel_id=1, source_target_pairs={{0,4},{1,5},{2,6},{3,7},{4,0},{5,1},{6,2},{7,3},{8,12},{9,13},{10,... | collective-permute-start | bytes 491528 | tf_op jit(solution)/shard_map/ppermute | solution.py:450
  9.5 1.2 copy-done.7
  10.7 1.2 copy-done.8
  11.9 1.6 shard_map.85
  14.4 2.8 %collective-permute-done.7.rest_2_ = bf16[8,80,128]{2,1,0:T(8,128)(2,1)S(1)} collective-permute-done((bf16[8,80,128]{2,1,0:T(8,128)(2,1)S(1)}, bf16[8,80,128]{2,1,0:T(8,128)(2,1)S(1)}, u32[]{:S(2)}, u32[]{:S(2)}) %collective-permute-start.7) | collective-permute-done | bytes 163872 | tf_op jit(solution)/shard_map/ppermute | solution.py:450
  17.2 2.3 %collective-permute-done.8.rest_3_ = bf16[8,80,128]{2,1,0:T(8,128)(2,1)S(1)} collective-permute-done((bf16[8,80,128]{2,1,0:T(8,128)(2,1)S(1)}, bf16[8,80,128]{2,1,0:T(8,128)(2,1)S(1)}, u32[]{:S(2)}, u32[]{:S(2)}) %collective-permute-start.8) | collective-permute-done | bytes 163872 | tf_op jit(solution)/shard_map/ppermute | solution.py:450
  19.5 1.6 shard_map.87
  21.2 7.0 %all-to-all-start = ((bf16[16,4,80,128]{3,2,1,0:T(8,128)(2,1)}), bf16[16,4,80,128]{3,2,1,0:T(8,128)(2,1)S(1)}, u32[]{:S(2)}, u32[]{:S(2)}) async-start(bf16[16,4,80,128]{3,2,1,0:T(8,128)(2,1)} %shard_map.87), calls=%async_computation | async-start | bytes 2621440 | tf_op jit(solution)/shard_map/all_to_all | solution.py:483
  28.3 1.4 collective-permute-start.4
  29.7 3.3 %collective-permute-start.5 = (bf16[128,1024]{1,0:T(8,128)(2,1)S(1)}, bf16[128,1024]{1,0:T(8,128)(2,1)S(1)}, u32[]{:S(2)}, u32[]{:S(2)}) collective-permute-start(bf16[128,1024]{1,0:T(8,128)(2,1)S(1)} %get-tuple-element.45), channel_id=1, source_target_pairs={{0,6},{1,7},{2,4},{3,5},{4,2},{5,3},{6,0},{7,1},{8,14},{9,15},{10,... | collective-permute-start | bytes 786440 | tf_op jit(solution)/shard_map/ppermute | solution.py:450
  33.0 1.6 collective-permute-start.11
  34.5 0.7 dynamic-slice_reduce_fusion.1
  35.3 0.8 constant_dynamic-slice_fusion
  36.7 0.8 select_reduce_fusion.3
  37.5 0.9 subtract_reduce_fusion
  38.6 5.7 %collective-permute-done.10.rest_2_ = bf16[8,80,128]{2,1,0:T(8,128)(2,1)S(1)} collective-permute-done((bf16[8,80,128]{2,1,0:T(8,128)(2,1)S(1)}, bf16[8,80,128]{2,1,0:T(8,128)(2,1)S(1)}, u32[]{:S(2)}, u32[]{:S(2)}) %collective-permute-start.10) | collective-permute-done | bytes 163872 | tf_op jit(solution)/shard_map/ppermute | solution.py:450
  44.6 5.8 %collective-permute-done.11.rest_3_ = bf16[8,80,128]{2,1,0:T(8,128)(2,1)S(1)} collective-permute-done((bf16[8,80,128]{2,1,0:T(8,128)(2,1)}, bf16[8,80,128]{2,1,0:T(8,128)(2,1)S(1)}, u32[]{:S(2)}, u32[]{:S(2)}) %collective-permute-start.11) | collective-permute-done | bytes 163872 | tf_op jit(solution)/shard_map/ppermute | solution.py:450
  50.5 1.7 shard_map.88.rest_0_
  53.0 4.4 %collective-permute-start.1 = (bf16[128,1024]{1,0:T(8,128)(2,1)}, bf16[128,1024]{1,0:T(8,128)(2,1)S(1)}, u32[]{:S(2)}, u32[]{:S(2)}) collective-permute-start(bf16[128,1024]{1,0:T(8,128)(2,1)} %get-tuple-element.41), channel_id=1, source_target_pairs={{0,4},{1,5},{2,6},{3,7},{4,0},{5,1},{6,2},{7,3},{8,12},{9,13},{10,... | collective-permute-start | bytes 786440 | tf_op jit(solution)/shard_map/ppermute | solution.py:450
  57.7 6.9 %all-to-all-start.1 = ((bf16[16,4,80,128]{3,2,1,0:T(8,128)(2,1)}), bf16[16,4,80,128]{3,2,1,0:T(8,128)(2,1)S(1)}, u32[]{:S(2)}, u32[]{:S(2)}) async-start(bf16[16,4,80,128]{3,2,1,0:T(8,128)(2,1)} %shard_map.88.rest_0_), calls=%async_computation.1 | async-start | bytes 2621440 | tf_op jit(solution)/shard_map/all_to_all | solution.py:483
  64.6 21.3 %shard_map.90 = (bf16[4,4,1024,640]{3,2,1,0:T(8,128)(2,1)}, f32[4,1024,128]{2,1,0:T(8,128)}) custom-call(s32[3,4]{1,0:T(4,128)} %copy-done.31, bf16[128,4096]{1,0:T(8,128)(2,1)} %bitcast.16, bf16[128,1024]{1,0:T(8,128)(2,1)} %copy-done.22, bf16[128,1024]{1,0:T(8,128)(2,1)} %copy-done.23, bf16[128,1024]{1,0:T(8,128)(2,1)} %copy-done.24, ...), custom_call_target="tpu_custom_call" | custom-call | flops 40265318400 | bytes 31457280 | tf_op jit(solution)/shard_map/pallas_call | solution.py:393
  85.9 1.8 copy-done.4
  88.5 2.1 %collective-permute-done.13.v_other = bf16[8,4,80,128]{3,2,1,0:T(8,128)(2,1)S(1)} collective-permute-done((bf16[8,4,80,128]{3,2,1,0:T(8,128)(2,1)S(1)}, bf16[8,4,80,128]{3,2,1,0:T(8,128)(2,1)S(1)}, u32[]{:S(2)}, u32[]{:S(2)}) %collective-permute-start.13) | collective-permute-done | bytes 655392 | tf_op jit(solution)/shard_map/ppermute | solution.py:450
  90.6 0.8 copy-done.37
  91.4 18.4 %shard_map.92 = (bf16[128,1024]{1,0:T(8,128)(2,1)}, bf16[128,1024]{1,0:T(8,128)(2,1)}, bf16[128,1024]{1,0:T(8,128)(2,1)}, bf16[128,1024]{1,0:T(8,128)(2,1)}, bf1...) custom-call(s32[3,4]{1,0:T(4,128)} %copy-done.31, ...), custom_call_target="tpu_custom_call" | custom-call | flops 40265318400 | bytes 31457280 | tf_op jit(solution)/shard_map/pallas_call | solution.py:412
  109.9 1.3 collective-permute-start.14
  111.2 3.2 %collective-permute-start.15 = (bf16[128,1024]{1,0:T(8,128)(2,1)}, bf16[128,1024]{1,0:T(8,128)(2,1)S(1)}, u32[]{:S(2)}, u32[]{:S(2)}) collective-permute-start(bf16[128,1024]{1,0:T(8,128)(2,1)} %get-tuple-element.58.a2), channel_id=1, source_target_pairs={{0,4},{1,5},{2,6},{3,7},{4,0},{5,1},{6,2},{7,3},{8,12},{9,13},{10,... | collective-permute-start | bytes 786440 | tf_op jit(solution)/shard_map/ppermute | solution.py:450
  114.7 1.3 copy-done.6
  116.0 1.7 shard_map.99
  117.7 12.4 %all-to-all-start.3 = ((bf16[16,4,80,128]{3,2,1,0:T(8,128)(2,1)}), bf16[16,4,80,128]{3,2,1,0:T(8,128)(2,1)S(1)}, u32[]{:S(2)}, u32[]{:S(2)}) async-start(bf16[16,4,80,128]{3,2,1,0:T(8,128)(2,1)} %shard_map.99), calls=%async_computation.3 | async-start | bytes 2621440 | tf_op jit(solution)/shard_map/all_to_all | solution.py:483
  130.1 24.1 %shard_map.94 = (bf16[128,1024]{1,0:T(8,128)(2,1)}, bf16[128,1024]{1,0:T(8,128)(2,1)}, bf16[128,1024]{1,0:T(8,128)(2,1)}, bf16[128,1024]{1,0:T(8,128)(2,1)}, f32...) custom-call(s32[3,4]{1,0:T(4,128)} %copy-done.31, bf16[128,4096]{1,0:T(8,128)(2,1)} %bitcast.17, ...), custom_call_target="tpu_custom_call" | custom-call | flops 60397977600 | bytes 31457280 | tf_op jit(solution)/shard_map/pallas_call | solution.py:428
  155.1 2.3 %collective-permute-done.20.b = bf16[8,4,80,128]{3,2,1,0:T(8,128)(2,1)S(1)} collective-permute-done((bf16[8,4,80,128]{3,2,1,0:T(8,128)(2,1)}, bf16[8,4,80,128]{3,2,1,0:T(8,128)(2,1)S(1)}, u32[]{:S(2)}, u32[]{:S(2)}) %collective-permute-start.20) | collective-permute-done | bytes 655392 | tf_op jit(solution)/shard_map/ppermute | solution.py:450
  158.1 1.0 copy-done.3
  159.1 9.7 %all-to-all-start.2 = ((bf16[16,4,80,128]{3,2,1,0:T(8,128)(2,1)}), bf16[16,4,80,128]{3,2,1,0:T(8,128)(2,1)S(1)}, u32[]{:S(2)}, u32[]{:S(2)}) async-start(bf16[16,4,80,128]{3,2,1,0:T(8,128)(2,1)} %copy-done.3), calls=%async_computation.2 | async-start | bytes 2621440 | tf_op jit(solution)/shard_map/all_to_all | solution.py:483
  168.9 4.4 %collective-permute-start.18 = (bf16[128,1024]{1,0:T(8,128)(2,1)}, bf16[128,1024]{1,0:T(8,128)(2,1)}, u32[]{:S(2)}, u32[]{:S(2)}) collective-permute-start(bf16[128,1024]{1,0:T(8,128)(2,1)} %get-tuple-element.63), channel_id=1, source_target_pairs={{0,4},{1,5},{2,6},{3,7},{4,0},{5,1},{6,2},{7,3},{8,12},{9,13},{10,... | collective-permute-start | bytes 786440 | tf_op jit(solution)/shard_map/ppermute | solution.py:450
  173.7 1.3 shard_map.100
  176.3 4.4 %collective-permute-start.26 = (bf16[8,80,128]{2,1,0:T(8,128)(2,1)}, bf16[8,80,128]{2,1,0:T(8,128)(2,1)S(1)}, u32[]{:S(2)}, u32[]{:S(2)}) collective-permute-start(bf16[8,80,128]{2,1,0:T(8,128)(2,1)} %get-tuple-element.75), channel_id=1, source_target_pairs={{0,4},{1,5},{2,6},{3,7},{4,0},{5,1},{6,2},{7,3},{8,12},{9,13},{10,... | collective-permute-start | bytes 491528 | tf_op jit(solution)/shard_map/ppermute | solution.py:450
  180.7 9.7 %all-to-all-done.2.s = bf16[16,4,80,128]{3,2,1,0:T(8,128)(2,1)S(1)} async-done(((bf16[16,4,80,128]{3,2,1,0:T(8,128)(2,1)}), bf16[16,4,80,128]{3,2,1,0:T(8,128)(2,1)S(1)}, u32[]{:S(2)}, u32[]{:S(2)}) %all-to-all-start.2) | async-done | bytes 1310752 | tf_op jit(solution)/shard_map/all_to_all | solution.py:483
  191.0 3.0 %collective-permute-start.27 = (bf16[8,80,128]{2,1,0:T(8,128)(2,1)S(1)}, bf16[8,80,128]{2,1,0:T(8,128)(2,1)S(1)}, u32[]{:S(2)}, u32[]{:S(2)}) collective-permute-start(bf16[8,80,128]{2,1,0:T(8,128)(2,1)S(1)} %copy-done.35), channel_id=1, source_target_pairs={{0,6},{1,7},{2,4},{3,5},{4,2},{5,3},{6,0},{7,1},{8,14},{9,15},{10,... | collective-permute-start | bytes 491528 | tf_op jit(solution)/shard_map/ppermute | solution.py:450
  194.0 1.8 collective-permute-start.22
  195.8 2.9 %collective-permute-start.23 = (bf16[8,80,128]{2,1,0:T(8,128)(2,1)S(1)}, bf16[8,80,128]{2,1,0:T(8,128)(2,1)S(1)}, u32[]{:S(2)}, u32[]{:S(2)}) collective-permute-start(bf16[8,80,128]{2,1,0:T(8,128)(2,1)S(1)} %get-tuple-element.70), channel_id=1, source_target_pairs={{0,6},{1,7},{2,4},{3,5},{4,2},{5,3},{6,0},{7,1},{8,14},{9,15},{10,... | collective-permute-start | bytes 491528 | tf_op jit(solution)/shard_map/ppermute | solution.py:450
  198.8 0.9 copy-done.17
  199.7 1.6 shard_map.93
  201.3 2.7 %shard_map.95 = bf16[128,4096]{1,0:T(8,128)(2,1)} custom-call(s32[4]{0:T(128)S(1)} %copy-done.28, bf16[128,1024]{1,0:T(8,128)(2,1)S(1)} %copy-done.18, bf16[128,1024]{1,0:T(8,128)(2,1)} %collective-permute-done.17.rest_1_, bf16[128,1024]{1,0:T(8,128)(2,1)} %collective-permute-done.18.rest_2_, bf16[128,1024]{1,0:T(8,128)(2,1)} %collective-permute-done.19.rest_3_), custom_call_target="tpu_custom_call" | custom-call | tf_op jit(solution)/shard_map/pallas_call | solution.py:42
  204.7 2.0 shard_map.101
  (120 shorter events, 9.3 us)
Async XLA Ops:
  0.6 33.9 %copy-start = (s32[16,8]{0,1:T(8,128)S(1)}, s32[16,8]{0,1:T(8,128)}, u32[]{:S(2)}) copy-start(s32[16,8]{0,1:T(8,128)} %param.11) | copy-start | bytes 1540
  1.2 12.4 %copy-start.27 = (s32[4]{0:T(128)}, s32[4]{0:T(128)S(1)}, u32[]{:S(2)}) copy-start(s32[4]{0:T(128)S(1)} %get-tuple-element.82.t) | copy-start | bytes 52
  2.5 7.0 %copy-start.2 = (bf16[1,8,80,1024]{3,2,1,0:T(8,128)(2,1)S(1)}, bf16[1,8,80,1024]{3,2,1,0:T(8,128)(2,1)}, u32[]{:S(2)}) copy-start(bf16[1,8,80,1024]{3,2,1,0:T(8,128)(2,1)} %param.8) | copy-start | bytes 3932164
  3.9 10.5 %collective-permute-start.6 = (bf16[8,80,128]{2,1,0:T(8,128)(2,1)}, bf16[8,80,128]{2,1,0:T(8,128)(2,1)S(1)}, u32[]{:S(2)}, u32[]{:S(2)}) collective-permute-start(bf16[8,80,128]{2,1,0:T(8,128)(2,1)} %get-tuple-element.47), channel_id=1, source_target_pairs={{0,2},{1,3},{2,0},{3,1},{4,6},{5,7},{6,4},{7,5},{8,10},{9,11},{10,... | collective-permute-start | bytes 491528 | tf_op jit(solution)/shard_map/ppermute | solution.py:450
  5.9 11.3 %collective-permute-start.7 = (bf16[8,80,128]{2,1,0:T(8,128)(2,1)S(1)}, bf16[8,80,128]{2,1,0:T(8,128)(2,1)S(1)}, u32[]{:S(2)}, u32[]{:S(2)}) collective-permute-start(bf16[8,80,128]{2,1,0:T(8,128)(2,1)S(1)} %get-tuple-element.48), channel_id=1, source_target_pairs={{0,4},{1,5},{2,6},{3,7},{4,0},{5,1},{6,2},{7,3},{8,12},{9,13},{10,... | collective-permute-start | bytes 491528 | tf_op jit(solution)/shard_map/ppermute | solution.py:450
  9.5 10.0 %collective-permute-start.8 = (bf16[8,80,128]{2,1,0:T(8,128)(2,1)S(1)}, bf16[8,80,128]{2,1,0:T(8,128)(2,1)S(1)}, u32[]{:S(2)}, u32[]{:S(2)}) collective-permute-start(bf16[8,80,128]{2,1,0:T(8,128)(2,1)S(1)} %get-tuple-element.49), channel_id=1, source_target_pairs={{0,6},{1,7},{2,4},{3,5},{4,2},{5,3},{6,0},{7,1},{8,14},{9,15},{10,... | collective-permute-start | bytes 491528 | tf_op jit(solution)/shard_map/ppermute | solution.py:450
  14.4 36.1 %copy-start.29 = (s32[8]{0:T(128)}, s32[8]{0:T(128)S(1)}, u32[]{:S(2)}) copy-start(s32[8]{0:T(128)S(1)} %select_reduce_fusion.t) | copy-start | bytes 100
  21.2 31.0 %all-to-all-start = ((bf16[16,4,80,128]{3,2,1,0:T(8,128)(2,1)}), bf16[16,4,80,128]{3,2,1,0:T(8,128)(2,1)S(1)}, u32[]{:S(2)}, u32[]{:S(2)}) async-start(bf16[16,4,80,128]{3,2,1,0:T(8,128)(2,1)} %shard_map.87), calls=%async_computation | async-start | bytes 2621440 | tf_op jit(solution)/shard_map/all_to_all | solution.py:483
  28.2 22.3 %collective-permute-start.3 = (bf16[128,1024]{1,0:T(8,128)(2,1)S(1)}, bf16[128,1024]{1,0:T(8,128)(2,1)S(1)}, u32[]{:S(2)}, u32[]{:S(2)}) collective-permute-start(bf16[128,1024]{1,0:T(8,128)(2,1)S(1)} %get-tuple-element.43), channel_id=1, source_target_pairs={{0,2},{1,3},{2,0},{3,1},{4,6},{5,7},{6,4},{7,5},{8,10},{9,11},{10,... | collective-permute-start | bytes 786440 | tf_op jit(solution)/shard_map/ppermute | solution.py:450
  28.3 22.2 %collective-permute-start.4 = (bf16[128,1024]{1,0:T(8,128)(2,1)S(1)}, bf16[128,1024]{1,0:T(8,128)(2,1)S(1)}, u32[]{:S(2)}, u32[]{:S(2)}) collective-permute-start(bf16[128,1024]{1,0:T(8,128)(2,1)S(1)} %get-tuple-element.44), channel_id=1, source_target_pairs={{0,4},{1,5},{2,6},{3,7},{4,0},{5,1},{6,2},{7,3},{8,12},{9,13},{10,... | collective-permute-start | bytes 786440 | tf_op jit(solution)/shard_map/ppermute | solution.py:450
  29.7 20.8 %collective-permute-start.5 = (bf16[128,1024]{1,0:T(8,128)(2,1)S(1)}, bf16[128,1024]{1,0:T(8,128)(2,1)S(1)}, u32[]{:S(2)}, u32[]{:S(2)}) collective-permute-start(bf16[128,1024]{1,0:T(8,128)(2,1)S(1)} %get-tuple-element.45), channel_id=1, source_target_pairs={{0,6},{1,7},{2,4},{3,5},{4,2},{5,3},{6,0},{7,1},{8,14},{9,15},{10,... | collective-permute-start | bytes 786440 | tf_op jit(solution)/shard_map/ppermute | solution.py:450
  33.0 11.4 %collective-permute-start.10 = (bf16[8,80,128]{2,1,0:T(8,128)(2,1)S(1)}, bf16[8,80,128]{2,1,0:T(8,128)(2,1)S(1)}, u32[]{:S(2)}, u32[]{:S(2)}) collective-permute-start(bf16[8,80,128]{2,1,0:T(8,128)(2,1)S(1)} %get-tuple-element.52), channel_id=1, source_target_pairs={{0,4},{1,5},{2,6},{3,7},{4,0},{5,1},{6,2},{7,3},{8,12},{9,13},{10,... | collective-permute-start | bytes 491528 | tf_op jit(solution)/shard_map/ppermute | solution.py:450
  33.0 17.5 %collective-permute-start.11 = (bf16[8,80,128]{2,1,0:T(8,128)(2,1)}, bf16[8,80,128]{2,1,0:T(8,128)(2,1)S(1)}, u32[]{:S(2)}, u32[]{:S(2)}) collective-permute-start(bf16[8,80,128]{2,1,0:T(8,128)(2,1)} %get-tuple-element.53), channel_id=1, source_target_pairs={{0,6},{1,7},{2,4},{3,5},{4,2},{5,3},{6,0},{7,1},{8,14},{9,15},{10,... | collective-permute-start | bytes 491528 | tf_op jit(solution)/shard_map/ppermute | solution.py:450
  44.3 6.1 %collective-permute-start.9 = (bf16[8,80,128]{2,1,0:T(8,128)(2,1)}, bf16[8,80,128]{2,1,0:T(8,128)(2,1)S(1)}, u32[]{:S(2)}, u32[]{:S(2)}) collective-permute-start(bf16[8,80,128]{2,1,0:T(8,128)(2,1)} %get-tuple-element.51), channel_id=1, source_target_pairs={{0,2},{1,3},{2,0},{3,1},{4,6},{5,7},{6,4},{7,5},{8,10},{9,11},{10,... | collective-permute-start | bytes 491528 | tf_op jit(solution)/shard_map/ppermute | solution.py:450
  44.6 7.6 %copy-start.31 = (s32[3,4]{1,0:T(4,128)}, s32[3,4]{1,0:T(4,128)S(1)}, u32[]{:S(2)}) copy-start(s32[3,4]{1,0:T(4,128)S(1)} %pad_add_fusion.rest_4_.info) | copy-start | bytes 148
  52.2 5.2 %copy-start.33 = (bf16[128,1024]{1,0:T(8,128)(2,1)S(1)}, bf16[128,1024]{1,0:T(8,128)(2,1)}, u32[]{:S(2)}) copy-start(bf16[128,1024]{1,0:T(8,128)(2,1)} %copy-done.32) | copy-start | bytes 786436
  52.8 4.9 %copy-start.16 = (bf16[8,4,80,128]{3,2,1,0:T(8,128)(2,1)}, bf16[8,4,80,128]{3,2,1,0:T(8,128)(2,1)S(1)}, u32[]{:S(2)}) copy-start(bf16[8,4,80,128]{3,2,1,0:T(8,128)(2,1)S(1)} %shard_map.89.k_mine) | copy-start | bytes 1966084
  52.8 11.7 %collective-permute-start.12 = (bf16[8,4,80,128]{3,2,1,0:T(8,128)(2,1)S(1)}, bf16[8,4,80,128]{3,2,1,0:T(8,128)(2,1)}, u32[]{:S(2)}, u32[]{:S(2)}) collective-permute-start(bf16[8,4,80,128]{3,2,1,0:T(8,128)(2,1)S(1)} %shard_map.89.k_mine), channel_id=1, source_target_pairs={{0,1},{1,0},{2,3},{3,2},{4,5},{5,4},{6,7},{7,6},{8,9},{9,8},{10,11... | collective-permute-start | bytes 1966088 | tf_op jit(solution)/shard_map/ppermute | solution.py:450
  52.9 32.9 %collective-permute-start = (bf16[128,1024]{1,0:T(8,128)(2,1)}, bf16[128,1024]{1,0:T(8,128)(2,1)S(1)}, u32[]{:S(2)}, u32[]{:S(2)}) collective-permute-start(bf16[128,1024]{1,0:T(8,128)(2,1)} %get-tuple-element.40), channel_id=1, source_target_pairs={{0,2},{1,3},{2,0},{3,1},{4,6},{5,7},{6,4},{7,5},{8,10},{9,11},{10,... | collective-permute-start | bytes 786440 | tf_op jit(solution)/shard_map/ppermute | solution.py:450
  53.0 32.9 %collective-permute-start.1 = (bf16[128,1024]{1,0:T(8,128)(2,1)}, bf16[128,1024]{1,0:T(8,128)(2,1)S(1)}, u32[]{:S(2)}, u32[]{:S(2)}) collective-permute-start(bf16[128,1024]{1,0:T(8,128)(2,1)} %get-tuple-element.41), channel_id=1, source_target_pairs={{0,4},{1,5},{2,6},{3,7},{4,0},{5,1},{6,2},{7,3},{8,12},{9,13},{10,... | collective-permute-start | bytes 786440 | tf_op jit(solution)/shard_map/ppermute | solution.py:450
  57.4 28.5 %collective-permute-start.2 = (bf16[128,1024]{1,0:T(8,128)(2,1)S(1)}, bf16[128,1024]{1,0:T(8,128)(2,1)S(1)}, u32[]{:S(2)}, u32[]{:S(2)}) collective-permute-start(bf16[128,1024]{1,0:T(8,128)(2,1)S(1)} %copy-done.33), channel_id=1, source_target_pairs={{0,6},{1,7},{2,4},{3,5},{4,2},{5,3},{6,0},{7,1},{8,14},{9,15},{10,... | collective-permute-start | bytes 786440 | tf_op jit(solution)/shard_map/ppermute | solution.py:450
  57.7 28.2 %all-to-all-start.1 = ((bf16[16,4,80,128]{3,2,1,0:T(8,128)(2,1)}), bf16[16,4,80,128]{3,2,1,0:T(8,128)(2,1)S(1)}, u32[]{:S(2)}, u32[]{:S(2)}) async-start(bf16[16,4,80,128]{3,2,1,0:T(8,128)(2,1)} %shard_map.88.rest_0_), calls=%async_computation.1 | async-start | bytes 2621440 | tf_op jit(solution)/shard_map/all_to_all | solution.py:483
  88.4 2.2 %collective-permute-start.13 = (bf16[8,4,80,128]{3,2,1,0:T(8,128)(2,1)S(1)}, bf16[8,4,80,128]{3,2,1,0:T(8,128)(2,1)S(1)}, u32[]{:S(2)}, u32[]{:S(2)}) collective-permute-start(bf16[8,4,80,128]{3,2,1,0:T(8,128)(2,1)S(1)} %shard_map.91.v_mine), channel_id=1, source_target_pairs={{0,1},{1,0},{2,3},{3,2},{4,5},{5,4},{6,7},{7,6},{8,9},{9,8},{10,11... | collective-permute-start | bytes 1966088 | tf_op jit(solution)/shard_map/ppermute | solution.py:450
  109.8 4.9 %collective-permute-start.24 = (bf16[8,4,80,128]{3,2,1,0:T(8,128)(2,1)}, bf16[8,4,80,128]{3,2,1,0:T(8,128)(2,1)S(1)}, u32[]{:S(2)}, u32[]{:S(2)}) collective-permute-start(bf16[8,4,80,128]{3,2,1,0:T(8,128)(2,1)} %get-tuple-element.72), channel_id=1, source_target_pairs={{0,1},{1,0},{2,3},{3,2},{4,5},{5,4},{6,7},{7,6},{8,9},{9,8},{10,11... | collective-permute-start | bytes 1966088 | tf_op jit(solution)/shard_map/ppermute | solution.py:450
  109.9 44.3 %collective-permute-start.14 = (bf16[128,1024]{1,0:T(8,128)(2,1)}, bf16[128,1024]{1,0:T(8,128)(2,1)S(1)}, u32[]{:S(2)}, u32[]{:S(2)}) collective-permute-start(bf16[128,1024]{1,0:T(8,128)(2,1)} %get-tuple-element.57.a1), channel_id=1, source_target_pairs={{0,2},{1,3},{2,0},{3,1},{4,6},{5,7},{6,4},{7,5},{8,10},{9,11},{10,... | collective-permute-start | bytes 786440 | tf_op jit(solution)/shard_map/ppermute | solution.py:450
  111.2 43.1 %collective-permute-start.15 = (bf16[128,1024]{1,0:T(8,128)(2,1)}, bf16[128,1024]{1,0:T(8,128)(2,1)S(1)}, u32[]{:S(2)}, u32[]{:S(2)}) collective-permute-start(bf16[128,1024]{1,0:T(8,128)(2,1)} %get-tuple-element.58.a2), channel_id=1, source_target_pairs={{0,4},{1,5},{2,6},{3,7},{4,0},{5,1},{6,2},{7,3},{8,12},{9,13},{10,... | collective-permute-start | bytes 786440 | tf_op jit(solution)/shard_map/ppermute | solution.py:450
  114.4 39.9 %collective-permute-start.16 = (bf16[128,1024]{1,0:T(8,128)(2,1)}, bf16[128,1024]{1,0:T(8,128)(2,1)S(1)}, u32[]{:S(2)}, u32[]{:S(2)}) collective-permute-start(bf16[128,1024]{1,0:T(8,128)(2,1)} %get-tuple-element.59.a3), channel_id=1, source_target_pairs={{0,6},{1,7},{2,4},{3,5},{4,2},{5,3},{6,0},{7,1},{8,14},{9,15},{10,... | collective-permute-start | bytes 786440 | tf_op jit(solution)/shard_map/ppermute | solution.py:450
  117.7 41.4 %all-to-all-start.3 = ((bf16[16,4,80,128]{3,2,1,0:T(8,128)(2,1)}), bf16[16,4,80,128]{3,2,1,0:T(8,128)(2,1)S(1)}, u32[]{:S(2)}, u32[]{:S(2)}) async-start(bf16[16,4,80,128]{3,2,1,0:T(8,128)(2,1)} %shard_map.99), calls=%async_computation.3 | async-start | bytes 2621440 | tf_op jit(solution)/shard_map/all_to_all | solution.py:483
  154.2 3.2 %copy-start.5 = (f32[8,4,80,128]{3,2,1,0:T(8,128)S(1)}, f32[8,4,80,128]{3,2,1,0:T(8,128)}, u32[]{:S(2)}) copy-start(f32[8,4,80,128]{3,2,1,0:T(8,128)} %get-tuple-element.65.a) | copy-start | bytes 3932164
  155.1 2.3 %collective-permute-start.20 = (bf16[8,4,80,128]{3,2,1,0:T(8,128)(2,1)}, bf16[8,4,80,128]{3,2,1,0:T(8,128)(2,1)S(1)}, u32[]{:S(2)}, u32[]{:S(2)}) collective-permute-start(bf16[8,4,80,128]{3,2,1,0:T(8,128)(2,1)} %shard_map.96), channel_id=1, source_target_pairs={{0,1},{1,0},{2,3},{3,2},{4,5},{5,4},{6,7},{7,6},{8,9},{9,8},{10,11... | collective-permute-start | bytes 1966088 | tf_op jit(solution)/shard_map/ppermute | solution.py:450
  159.1 14.5 %copy-start.30 = (s32[8]{0:T(128)S(1)}, s32[8]{0:T(128)}, u32[]{:S(2)}) copy-start(s32[8]{0:T(128)} %copy-done.29) | copy-start | bytes 100
  159.1 31.3 %all-to-all-start.2 = ((bf16[16,4,80,128]{3,2,1,0:T(8,128)(2,1)}), bf16[16,4,80,128]{3,2,1,0:T(8,128)(2,1)S(1)}, u32[]{:S(2)}, u32[]{:S(2)}) async-start(bf16[16,4,80,128]{3,2,1,0:T(8,128)(2,1)} %copy-done.3), calls=%async_computation.2 | async-start | bytes 2621440 | tf_op jit(solution)/shard_map/all_to_all | solution.py:483
  168.8 22.2 %collective-permute-start.17 = (bf16[128,1024]{1,0:T(8,128)(2,1)}, bf16[128,1024]{1,0:T(8,128)(2,1)}, u32[]{:S(2)}, u32[]{:S(2)}) collective-permute-start(bf16[128,1024]{1,0:T(8,128)(2,1)} %get-tuple-element.62), channel_id=1, source_target_pairs={{0,2},{1,3},{2,0},{3,1},{4,6},{5,7},{6,4},{7,5},{8,10},{9,11},{10,... | collective-permute-start | bytes 786440 | tf_op jit(solution)/shard_map/ppermute | solution.py:450
  168.9 25.1 %collective-permute-start.18 = (bf16[128,1024]{1,0:T(8,128)(2,1)}, bf16[128,1024]{1,0:T(8,128)(2,1)}, u32[]{:S(2)}, u32[]{:S(2)}) collective-permute-start(bf16[128,1024]{1,0:T(8,128)(2,1)} %get-tuple-element.63), channel_id=1, source_target_pairs={{0,4},{1,5},{2,6},{3,7},{4,0},{5,1},{6,2},{7,3},{8,12},{9,13},{10,... | collective-permute-start | bytes 786440 | tf_op jit(solution)/shard_map/ppermute | solution.py:450
  173.3 25.4 %copy-start.10 = (bf16[128,1024]{1,0:T(8,128)(2,1)S(1)}, bf16[128,1024]{1,0:T(8,128)(2,1)}, u32[]{:S(2)}) copy-start(bf16[128,1024]{1,0:T(8,128)(2,1)} %copy-done.9) | copy-start | bytes 786436
  173.3 25.5 %copy-start.12 = (bf16[128,1024]{1,0:T(8,128)(2,1)S(1)}, bf16[128,1024]{1,0:T(8,128)(2,1)}, u32[]{:S(2)}) copy-start(bf16[128,1024]{1,0:T(8,128)(2,1)} %copy-done.11) | copy-start | bytes 786436
  173.3 25.5 %copy-start.14 = (bf16[128,1024]{1,0:T(8,128)(2,1)S(1)}, bf16[128,1024]{1,0:T(8,128)(2,1)}, u32[]{:S(2)}) copy-start(bf16[128,1024]{1,0:T(8,128)(2,1)} %copy-done.13) | copy-start | bytes 786436
  173.3 25.5 %copy-start.28 = (s32[4]{0:T(128)S(1)}, s32[4]{0:T(128)}, u32[]{:S(2)}) copy-start(s32[4]{0:T(128)} %copy-done.27) | copy-start | bytes 52
  173.3 20.7 %collective-permute-start.19 = (bf16[128,1024]{1,0:T(8,128)(2,1)}, bf16[128,1024]{1,0:T(8,128)(2,1)}, u32[]{:S(2)}, u32[]{:S(2)}) collective-permute-start(bf16[128,1024]{1,0:T(8,128)(2,1)} %get-tuple-element.64), channel_id=1, source_target_pairs={{0,6},{1,7},{2,4},{3,5},{4,2},{5,3},{6,0},{7,1},{8,14},{9,15},{10,... | collective-permute-start | bytes 786440 | tf_op jit(solution)/shard_map/ppermute | solution.py:450
  176.3 14.7 %copy-start.35 = (bf16[8,80,128]{2,1,0:T(8,128)(2,1)S(1)}, bf16[8,80,128]{2,1,0:T(8,128)(2,1)}, u32[]{:S(2)}) copy-start(bf16[8,80,128]{2,1,0:T(8,128)(2,1)} %copy-done.34) | copy-start | bytes 491524
  176.3 19.5 %collective-permute-start.25 = (bf16[8,80,128]{2,1,0:T(8,128)(2,1)}, bf16[8,80,128]{2,1,0:T(8,128)(2,1)S(1)}, u32[]{:S(2)}, u32[]{:S(2)}) collective-permute-start(bf16[8,80,128]{2,1,0:T(8,128)(2,1)} %get-tuple-element.74), channel_id=1, source_target_pairs={{0,2},{1,3},{2,0},{3,1},{4,6},{5,7},{6,4},{7,5},{8,10},{9,11},{10,... | collective-permute-start | bytes 491528 | tf_op jit(solution)/shard_map/ppermute | solution.py:450
  176.3 27.7 %collective-permute-start.26 = (bf16[8,80,128]{2,1,0:T(8,128)(2,1)}, bf16[8,80,128]{2,1,0:T(8,128)(2,1)S(1)}, u32[]{:S(2)}, u32[]{:S(2)}) collective-permute-start(bf16[8,80,128]{2,1,0:T(8,128)(2,1)} %get-tuple-element.75), channel_id=1, source_target_pairs={{0,4},{1,5},{2,6},{3,7},{4,0},{5,1},{6,2},{7,3},{8,12},{9,13},{10,... | collective-permute-start | bytes 491528 | tf_op jit(solution)/shard_map/ppermute | solution.py:450
  190.4 10.9 %copy-start.18 = (bf16[128,1024]{1,0:T(8,128)(2,1)S(1)}, bf16[128,1024]{1,0:T(8,128)(2,1)}, u32[]{:S(2)}) copy-start(bf16[128,1024]{1,0:T(8,128)(2,1)} %get-tuple-element.61.rest_0_) | copy-start | bytes 786436
  191.0 13.0 %collective-permute-start.27 = (bf16[8,80,128]{2,1,0:T(8,128)(2,1)S(1)}, bf16[8,80,128]{2,1,0:T(8,128)(2,1)S(1)}, u32[]{:S(2)}, u32[]{:S(2)}) collective-permute-start(bf16[8,80,128]{2,1,0:T(8,128)(2,1)S(1)} %copy-done.35), channel_id=1, source_target_pairs={{0,6},{1,7},{2,4},{3,5},{4,2},{5,3},{6,0},{7,1},{8,14},{9,15},{10,... | collective-permute-start | bytes 491528 | tf_op jit(solution)/shard_map/ppermute | solution.py:450
  194.0 10.0 %collective-permute-start.21 = (bf16[8,80,128]{2,1,0:T(8,128)(2,1)S(1)}, bf16[8,80,128]{2,1,0:T(8,128)(2,1)S(1)}, u32[]{:S(2)}, u32[]{:S(2)}) collective-permute-start(bf16[8,80,128]{2,1,0:T(8,128)(2,1)S(1)} %get-tuple-element.68), channel_id=1, source_target_pairs={{0,2},{1,3},{2,0},{3,1},{4,6},{5,7},{6,4},{7,5},{8,10},{9,11},{10,... | collective-permute-start | bytes 491528 | tf_op jit(solution)/shard_map/ppermute | solution.py:450
  194.0 10.0 %collective-permute-start.22 = (bf16[8,80,128]{2,1,0:T(8,128)(2,1)S(1)}, bf16[8,80,128]{2,1,0:T(8,128)(2,1)S(1)}, u32[]{:S(2)}, u32[]{:S(2)}) collective-permute-start(bf16[8,80,128]{2,1,0:T(8,128)(2,1)S(1)} %get-tuple-element.69), channel_id=1, source_target_pairs={{0,4},{1,5},{2,6},{3,7},{4,0},{5,1},{6,2},{7,3},{8,12},{9,13},{10,... | collective-permute-start | bytes 491528 | tf_op jit(solution)/shard_map/ppermute | solution.py:450
  195.8 8.8 %collective-permute-start.23 = (bf16[8,80,128]{2,1,0:T(8,128)(2,1)S(1)}, bf16[8,80,128]{2,1,0:T(8,128)(2,1)S(1)}, u32[]{:S(2)}, u32[]{:S(2)}) collective-permute-start(bf16[8,80,128]{2,1,0:T(8,128)(2,1)S(1)} %get-tuple-element.70), channel_id=1, source_target_pairs={{0,6},{1,7},{2,4},{3,5},{4,2},{5,3},{6,0},{7,1},{8,14},{9,15},{10,... | collective-permute-start | bytes 491528 | tf_op jit(solution)/shard_map/ppermute | solution.py:450
  201.3 3.4 %copy-start.26 = (bf16[8,80,128]{2,1,0:T(8,128)(2,1)S(1)}, bf16[8,80,128]{2,1,0:T(8,128)(2,1)}, u32[]{:S(2)}) copy-start(bf16[8,80,128]{2,1,0:T(8,128)(2,1)} %copy-done.25) | copy-start | bytes 491524
  (22 other events, 31.3 us)
where the time goes:
time: 207 us
  Pallas kernels  81.8 us (40%)
  starting transfers between devices  74.6 us (36%)
  waiting for transfers between devices  31.4 us (15%)
  local copies, waits for them, and re-layouts  14.4 us (7%)
  other arithmetic  3.28 us (2%)
    ppermute x28, starting transfers between devices, swap(): return lax.ppermute(x, 'seq', [(i, i ^ mask) for i in range(N_SEQ)])  38.7 us
    all_to_all x4, starting transfers between devices, exchange(): return lax.all_to_all(x, 'dp', split_axis=0, concat_axis=0, tiled=True)  35.9 us
    pallas_call x1, Pallas kernels, gradients(): attention_call(grads_body, 3, TEXT_OUT + TILES_OUT, TEXT + [by_block(*E_S...  24.1 us
    ppermute x28, waiting for transfers between devices, swap(): return lax.ppermute(x, 'seq', [(i, i ^ mask) for i in range(N_SEQ)])  21.8 us
    pallas_call x1, Pallas kernels, weights(): attention_call(weights_body, 2, (struct(CHIPS, *E_SHAPE), jax.ShapeDtypeS...  21.3 us
    pallas_call x1, Pallas kernels, outputs(): attention_call(outputs_body, 2, TEXT_OUT + (struct(CHIPS, *D_SHAPE),) + T...  18.4 us
    pallas_call x11, Pallas kernels, copier(): pl.pallas_call(body, out_shape=shapes, grid_spec=pltpu.PrefetchScalarGrid...  15 us
    unnamed x76, local copies, waits for them, and re-layouts  12.7 us
  transfers between devices with their start and end apart: 32, of which 8 were waited for; matrix products, arithmetic and copies ran while one was open for 2% of the time, Pallas kernels for 28%

commit v1 on v0

--- a/solution.py
+++ b/solution.py
@@ -24,6 +24,7 @@
 PIECE = (TPS, ROWS, HD)
 PIECES = (TPS, CHIPS, ROWS, HD)
 EXP_SCALE = SCALE * 1.4426950408889634
+LONG = 10**11
 BF = jnp.bfloat16
 F32 = jnp.float32
 
@@ -38,7 +39,7 @@
     return pl.BlockSpec(shape, lambda i, t: zeros)
 
 
-def copier(body, shapes, table, *arrays, after=()):
+def copier(body, shapes, table, *arrays, after=(), flops=0):
     return pl.pallas_call(
         body,
         out_shape=shapes,
@@ -50,6 +51,7 @@
             out_specs=jax.tree.map(lambda a: whole(a.shape), shapes),
         ),
         compiler_params=pltpu.CompilerParams(vmem_limit_bytes=32 * 2**20),
+        cost_estimate=pl.CostEstimate(flops=flops, bytes_accessed=2**22, transcendentals=0),
     )(table, *arrays, *after)
 
 
@@ -107,12 +109,12 @@
     return copier(body, struct(16, *PIECES[1:]), group_of, *pieces, after=after)
 
 
-def chosen(table, arrived, *after):
+def chosen(table, arrived, *after, flops=0):
     def body(t, s, *rest):
         for j in range(TPS):
             rest[-1][j] = s[t[j]]
 
-    return copier(body, struct(*PIECES), table, arrived, after=after)
+    return copier(body, struct(*PIECES), table, arrived, after=after, flops=flops)
 
 
 def outgoing_sums(owner, own, other):
@@ -360,7 +362,7 @@
 W_SHAPE = (LINES, HD)
 
 
-def attention_call(body, matmuls, out_shape, in_specs, out_specs, scratch_shapes):
+def attention_call(body, work, out_shape, in_specs, out_specs, scratch_shapes):
     return pl.pallas_call(
         body,
         out_shape=out_shape,
@@ -373,8 +375,8 @@
         ),
         compiler_params=pltpu.CompilerParams(vmem_limit_bytes=56 * 2**20),
         cost_estimate=pl.CostEstimate(
-            flops=20 * matmuls * LINES * CHIPS * 3 * TT * HD,
-            bytes_accessed=30 * 2**20,
+            flops=work * 10**9,
+            bytes_accessed=work * 2**20,
             transcendentals=0,
         ),
     )
@@ -392,7 +394,7 @@
 def weights(info, queries, tiles):
     return attention_call(
         weights_body,
-        2,
+        0,
         (struct(CHIPS, *E_SHAPE), jax.ShapeDtypeStruct((CHIPS,) + W_SHAPE, F32)),
         TEXT + TILES,
         (by_block(*E_SHAPE), by_block(*W_SHAPE)),
@@ -411,7 +413,7 @@
 def outputs(info, grads, e, w, tiles):
     return attention_call(
         outputs_body,
-        2,
+        40,
         TEXT_OUT + (struct(CHIPS, *D_SHAPE),) + TILES_OUT,
         TEXT + [by_block(*E_SHAPE), by_block(*W_SHAPE)] + TILES,
         TEXT_KEPT + (by_block(*D_SHAPE),) + TILES_KEPT,
@@ -427,7 +429,7 @@
 def gradients(info, queries, e, d, attn, keys, values):
     return attention_call(
         grads_body,
-        3,
+        60,
         TEXT_OUT + TILES_OUT,
         TEXT
         + [by_block(*E_SHAPE), by_block(*D_SHAPE)]
@@ -488,11 +490,11 @@
     q_text = spread([queries, *texts[:3]])
     g_text = spread([grad_out, *texts[3:]])
     keys = exchange(outgoing_pieces(group_of, spread(k_pieces), v_pieces[0]))
-    values = outgoing_pieces(group_of, spread(v_pieces), info, *q_text[1:])
-    keys = chosen(owner, keys, values)
+    values = outgoing_pieces(group_of, spread(v_pieces), info)
+    keys = chosen(owner, keys, values, *q_text[1:], flops=LONG)
     keys = keys, swap(keys, 1)
     e, w = weights(info, q_text, keys)
-    values = chosen(owner, exchange(values), w, *g_text[1:])
+    values = chosen(owner, exchange(values), e, *g_text[1:])
     values = values, swap(values, 1)
 
     *attn, d, dv_mine, dv_other = outputs(info, g_text, e, w, values)

time: 207 us -> 201 us (0.971)
  Pallas kernels: 81.8 us -> 76.7 us
  other arithmetic: 3.28 us -> 0.79 us
    pallas_call x3, Pallas kernels: 63.8 us -> 59.3 us  [the longest x1 22 us: gradients(): attention_call(grads_body, 60, TEXT_OUT + TILES_OUT, TEXT + [by_block(*E_...]
    unnamed x76 -> x84, local copies, waits for them, and re-layouts: 12.7 us -> 13.7 us
  transfers between devices with their start and end apart: 32 -> 32, of which waited for: 8 -> 9; matrix products, arithmetic and copies ran while one was open for 2% -> 1% of each run, Pallas kernels for 28% -> 27%
where the time goes in v1:
time: 201 us; the launch traced here: 199 us
  Pallas kernels  76.7 us (38%)
  starting transfers between devices  75.2 us (37%)
  waiting for transfers between devices  31.1 us (15%)
  local copies, waits for them, and re-layouts  14.1 us (7%)
    ppermute x28, starting transfers between devices, swap(): return lax.ppermute(x, 'seq', [(i, i ^ mask) for i in range(N_SEQ)])  37.7 us
    all_to_all x4, starting transfers between devices, exchange(): return lax.all_to_all(x, 'dp', split_axis=0, concat_axis=0, tiled=True)  37.5 us
    pallas_call x1, Pallas kernels, gradients(): attention_call(grads_body, 60, TEXT_OUT + TILES_OUT, TEXT + [by_block(*E_...  22 us
    ppermute x28, waiting for transfers between devices, swap(): return lax.ppermute(x, 'seq', [(i, i ^ mask) for i in range(N_SEQ)])  21 us
    pallas_call x1, Pallas kernels, weights(): attention_call(weights_body, 0, (struct(CHIPS, *E_SHAPE), jax.ShapeDtypeS...  19 us
    pallas_call x1, Pallas kernels, outputs(): attention_call(outputs_body, 40, TEXT_OUT + (struct(CHIPS, *D_SHAPE),) +...  18.3 us
    pallas_call x11, Pallas kernels, copier(): pl.pallas_call(body, out_shape=shapes, grid_spec=pltpu.PrefetchScalarGrid...  15.1 us
    unnamed x84, local copies, waits for them, and re-layouts  13.7 us
  transfers between devices with their start and end apart: 32, of which 9 were waited for; matrix products, arithmetic and copies ran while one was open for 1% of the time, Pallas kernels for 27%

profile of v1, /device:TPU:0, one launch (start us, length us, event | category | flops | bytes accessed | tf_op | source)
XLA Modules:
  0.0 199.0 jit_solution(13712147975936048258)
XLA Ops:
  0.7 1.3 copy-done.1
  2.7 2.1 %collective-permute-start.6 = (bf16[8,80,128]{2,1,0:T(8,128)(2,1)S(1)}, bf16[8,80,128]{2,1,0:T(8,128)(2,1)S(1)}, u32[]{:S(2)}, u32[]{:S(2)}) collective-permute-start(bf16[8,80,128]{2,1,0:T(8,128)(2,1)S(1)} %get-tuple-element.47), channel_id=1, source_target_pairs={{0,2},{1,3},{2,0},{3,1},{4,6},{5,7},{6,4},{7,5},{8,10},{9,11},{10,... | collective-permute-start | bytes 491528 | tf_op jit(solution)/shard_map/ppermute | solution.py:452
  4.8 3.6 %collective-permute-start.7 = (bf16[8,80,128]{2,1,0:T(8,128)(2,1)S(1)}, bf16[8,80,128]{2,1,0:T(8,128)(2,1)S(1)}, u32[]{:S(2)}, u32[]{:S(2)}) collective-permute-start(bf16[8,80,128]{2,1,0:T(8,128)(2,1)S(1)} %get-tuple-element.48), channel_id=1, source_target_pairs={{0,4},{1,5},{2,6},{3,7},{4,0},{5,1},{6,2},{7,3},{8,12},{9,13},{10,... | collective-permute-start | bytes 491528 | tf_op jit(solution)/shard_map/ppermute | solution.py:452
  8.4 1.2 copy-done.4
  9.6 1.2 copy-done.7
  10.8 1.6 shard_map.85
  13.2 0.7 copy-done.32
  14.7 1.2 collective-permute-done.7.rest_2_
  15.9 2.4 %collective-permute-done.8.rest_3_ = bf16[8,80,128]{2,1,0:T(8,128)(2,1)S(1)} collective-permute-done((bf16[8,80,128]{2,1,0:T(8,128)(2,1)S(1)}, bf16[8,80,128]{2,1,0:T(8,128)(2,1)S(1)}, u32[]{:S(2)}, u32[]{:S(2)}) %collective-permute-start.8) | collective-permute-done | bytes 163872 | tf_op jit(solution)/shard_map/ppermute | solution.py:452
  18.3 1.6 shard_map.87
  20.0 7.2 %all-to-all-start = ((bf16[16,4,80,128]{3,2,1,0:T(8,128)(2,1)}), bf16[16,4,80,128]{3,2,1,0:T(8,128)(2,1)S(1)}, u32[]{:S(2)}, u32[]{:S(2)}) async-start(bf16[16,4,80,128]{3,2,1,0:T(8,128)(2,1)} %shard_map.87), calls=%async_computation | async-start | bytes 2621440 | tf_op jit(solution)/shard_map/all_to_all | solution.py:485
  27.2 1.4 collective-permute-start.11
  28.6 2.1 %collective-permute-start.3 = (bf16[128,1024]{1,0:T(8,128)(2,1)}, bf16[128,1024]{1,0:T(8,128)(2,1)S(1)}, u32[]{:S(2)}, u32[]{:S(2)}) collective-permute-start(bf16[128,1024]{1,0:T(8,128)(2,1)} %get-tuple-element.43), channel_id=1, source_target_pairs={{0,2},{1,3},{2,0},{3,1},{4,6},{5,7},{6,4},{7,5},{8,10},{9,11},{10,... | collective-permute-start | bytes 786440 | tf_op jit(solution)/shard_map/ppermute | solution.py:452
  30.7 1.3 collective-permute-start.4
  32.0 1.4 collective-permute-start.5
  34.2 1.6 collective-permute-done.10.rest_2_
  36.1 1.7 collective-permute-done.11.rest_3_
  37.8 8.7 %collective-permute-done.9.rest_1_ = bf16[8,80,128]{2,1,0:T(8,128)(2,1)S(1)} collective-permute-done((bf16[8,80,128]{2,1,0:T(8,128)(2,1)}, bf16[8,80,128]{2,1,0:T(8,128)(2,1)S(1)}, u32[]{:S(2)}, u32[]{:S(2)}) %collective-permute-start.9) | collective-permute-done | bytes 163872 | tf_op jit(solution)/shard_map/ppermute | solution.py:452
  46.5 1.7 shard_map.88.rest_0_
  48.2 6.9 %all-to-all-start.1 = ((bf16[16,4,80,128]{3,2,1,0:T(8,128)(2,1)}), bf16[16,4,80,128]{3,2,1,0:T(8,128)(2,1)S(1)}, u32[]{:S(2)}, u32[]{:S(2)}) async-start(bf16[16,4,80,128]{3,2,1,0:T(8,128)(2,1)} %shard_map.88.rest_0_), calls=%async_computation.1 | async-start | bytes 2621440 | tf_op jit(solution)/shard_map/all_to_all | solution.py:485
  56.1 1.1 collective-permute-start
  57.2 2.9 %collective-permute-start.1 = (bf16[128,1024]{1,0:T(8,128)(2,1)S(1)}, bf16[128,1024]{1,0:T(8,128)(2,1)S(1)}, u32[]{:S(2)}, u32[]{:S(2)}) collective-permute-start(bf16[128,1024]{1,0:T(8,128)(2,1)S(1)} %copy-done.33), channel_id=1, source_target_pairs={{0,4},{1,5},{2,6},{3,7},{4,0},{5,1},{6,2},{7,3},{8,12},{9,13},{10,... | collective-permute-start | bytes 786440 | tf_op jit(solution)/shard_map/ppermute | solution.py:452
  60.8 0.8 copy-done.38
  61.7 19.0 %shard_map.90 = (bf16[4,4,1024,640]{3,2,1,0:T(8,128)(2,1)}, f32[4,1024,128]{2,1,0:T(8,128)}) custom-call(s32[3,4]{1,0:T(4,128)} %copy-done.25, bf16[128,4096]{1,0:T(8,128)(2,1)} %bitcast.14, bf16[128,1024]{1,0:T(8,128)(2,1)} %copy-done.21, bf16[128,1024]{1,0:T(8,128)(2,1)} %copy-done.22, bf16[128,1024]{1,0:T(8,128)(2,1)} %collective-permute-done.5.rest_3_.q3, ...), custom_call_target="tpu_custom_call" | custom-call | tf_op jit(solution)/shard_map/pallas_call | solution.py:395
  81.6 2.1 %collective-permute-done.13.v_other = bf16[8,4,80,128]{3,2,1,0:T(8,128)(2,1)S(1)} collective-permute-done((bf16[8,4,80,128]{3,2,1,0:T(8,128)(2,1)S(1)}, bf16[8,4,80,128]{3,2,1,0:T(8,128)(2,1)S(1)}, u32[]{:S(2)}, u32[]{:S(2)}) %collective-permute-start.13) | collective-permute-done | bytes 655392 | tf_op jit(solution)/shard_map/ppermute | solution.py:452
  83.7 0.8 copy-done.41
  84.5 18.3 %shard_map.92 = (bf16[128,1024]{1,0:T(8,128)(2,1)}, bf16[128,1024]{1,0:T(8,128)(2,1)}, bf16[128,1024]{1,0:T(8,128)(2,1)}, bf16[128,1024]{1,0:T(8,128)(2,1)}, bf1...) custom-call(s32[3,4]{1,0:T(4,128)} %copy-done.25, ...), custom_call_target="tpu_custom_call" | custom-call | flops 40000000000 | bytes 41943040 | tf_op jit(solution)/shard_map/pallas_call | solution.py:414
  103.0 4.0 %collective-permute-start.15 = (bf16[128,1024]{1,0:T(8,128)(2,1)}, bf16[128,1024]{1,0:T(8,128)(2,1)S(1)}, u32[]{:S(2)}, u32[]{:S(2)}) collective-permute-start(bf16[128,1024]{1,0:T(8,128)(2,1)} %get-tuple-element.58.a2), channel_id=1, source_target_pairs={{0,4},{1,5},{2,6},{3,7},{4,0},{5,1},{6,2},{7,3},{8,12},{9,13},{10,... | collective-permute-start | bytes 786440 | tf_op jit(solution)/shard_map/ppermute | solution.py:452
  107.7 1.3 copy-done.6
  109.0 1.8 shard_map.99
  110.7 13.4 %all-to-all-start.3 = ((bf16[16,4,80,128]{3,2,1,0:T(8,128)(2,1)}), bf16[16,4,80,128]{3,2,1,0:T(8,128)(2,1)S(1)}, u32[]{:S(2)}, u32[]{:S(2)}) async-start(bf16[16,4,80,128]{3,2,1,0:T(8,128)(2,1)} %shard_map.99), calls=%async_computation.3 | async-start | bytes 2621440 | tf_op jit(solution)/shard_map/all_to_all | solution.py:485
  124.1 22.0 %shard_map.94 = (bf16[128,1024]{1,0:T(8,128)(2,1)}, bf16[128,1024]{1,0:T(8,128)(2,1)}, bf16[128,1024]{1,0:T(8,128)(2,1)}, bf16[128,1024]{1,0:T(8,128)(2,1)}, f32...) custom-call(s32[3,4]{1,0:T(4,128)} %copy-done.25, bf16[128,4096]{1,0:T(8,128)(2,1)} %bitcast.15, ...), custom_call_target="tpu_custom_call" | custom-call | flops 60000002048 | bytes 62914560 | tf_op jit(solution)/shard_map/pallas_call | solution.py:430
  147.0 2.3 %collective-permute-done.20.b = bf16[8,4,80,128]{3,2,1,0:T(8,128)(2,1)S(1)} collective-permute-done((bf16[8,4,80,128]{3,2,1,0:T(8,128)(2,1)}, bf16[8,4,80,128]{3,2,1,0:T(8,128)(2,1)S(1)}, u32[]{:S(2)}, u32[]{:S(2)}) %collective-permute-start.20) | collective-permute-done | bytes 655392 | tf_op jit(solution)/shard_map/ppermute | solution.py:452
  150.0 1.0 copy-done.3
  151.1 10.1 %all-to-all-start.2 = ((bf16[16,4,80,128]{3,2,1,0:T(8,128)(2,1)}), bf16[16,4,80,128]{3,2,1,0:T(8,128)(2,1)S(1)}, u32[]{:S(2)}, u32[]{:S(2)}) async-start(bf16[16,4,80,128]{3,2,1,0:T(8,128)(2,1)} %copy-done.3), calls=%async_computation.2 | async-start | bytes 2621440 | tf_op jit(solution)/shard_map/all_to_all | solution.py:485
  161.2 4.0 %collective-permute-start.18 = (bf16[128,1024]{1,0:T(8,128)(2,1)}, bf16[128,1024]{1,0:T(8,128)(2,1)}, u32[]{:S(2)}, u32[]{:S(2)}) collective-permute-start(bf16[128,1024]{1,0:T(8,128)(2,1)} %get-tuple-element.63), channel_id=1, source_target_pairs={{0,4},{1,5},{2,6},{3,7},{4,0},{5,1},{6,2},{7,3},{8,12},{9,13},{10,... | collective-permute-start | bytes 786440 | tf_op jit(solution)/shard_map/ppermute | solution.py:452
  165.2 0.8 collective-permute-start.19
  166.0 1.3 shard_map.100
  168.6 4.0 %collective-permute-start.26 = (bf16[8,80,128]{2,1,0:T(8,128)(2,1)}, bf16[8,80,128]{2,1,0:T(8,128)(2,1)S(1)}, u32[]{:S(2)}, u32[]{:S(2)}) collective-permute-start(bf16[8,80,128]{2,1,0:T(8,128)(2,1)} %get-tuple-element.75), channel_id=1, source_target_pairs={{0,4},{1,5},{2,6},{3,7},{4,0},{5,1},{6,2},{7,3},{8,12},{9,13},{10,... | collective-permute-start | bytes 491528 | tf_op jit(solution)/shard_map/ppermute | solution.py:452
  172.7 10.1 %all-to-all-done.2.s = bf16[16,4,80,128]{3,2,1,0:T(8,128)(2,1)S(1)} async-done(((bf16[16,4,80,128]{3,2,1,0:T(8,128)(2,1)}), bf16[16,4,80,128]{3,2,1,0:T(8,128)(2,1)S(1)}, u32[]{:S(2)}, u32[]{:S(2)}) %all-to-all-start.2) | async-done | bytes 1310752 | tf_op jit(solution)/shard_map/all_to_all | solution.py:485
  183.3 2.6 %collective-permute-start.27 = (bf16[8,80,128]{2,1,0:T(8,128)(2,1)S(1)}, bf16[8,80,128]{2,1,0:T(8,128)(2,1)S(1)}, u32[]{:S(2)}, u32[]{:S(2)}) collective-permute-start(bf16[8,80,128]{2,1,0:T(8,128)(2,1)S(1)} %copy-done.37), channel_id=1, source_target_pairs={{0,6},{1,7},{2,4},{3,5},{4,2},{5,3},{6,0},{7,1},{8,14},{9,15},{10,... | collective-permute-start | bytes 491528 | tf_op jit(solution)/shard_map/ppermute | solution.py:452
  186.0 2.1 %collective-permute-start.22 = (bf16[8,80,128]{2,1,0:T(8,128)(2,1)S(1)}, bf16[8,80,128]{2,1,0:T(8,128)(2,1)S(1)}, u32[]{:S(2)}, u32[]{:S(2)}) collective-permute-start(bf16[8,80,128]{2,1,0:T(8,128)(2,1)S(1)} %get-tuple-element.69), channel_id=1, source_target_pairs={{0,4},{1,5},{2,6},{3,7},{4,0},{5,1},{6,2},{7,3},{8,12},{9,13},{10,... | collective-permute-start | bytes 491528 | tf_op jit(solution)/shard_map/ppermute | solution.py:452
  188.1 2.6 %collective-permute-start.23 = (bf16[8,80,128]{2,1,0:T(8,128)(2,1)S(1)}, bf16[8,80,128]{2,1,0:T(8,128)(2,1)S(1)}, u32[]{:S(2)}, u32[]{:S(2)}) collective-permute-start(bf16[8,80,128]{2,1,0:T(8,128)(2,1)S(1)} %get-tuple-element.70), channel_id=1, source_target_pairs={{0,6},{1,7},{2,4},{3,5},{4,2},{5,3},{6,0},{7,1},{8,14},{9,15},{10,... | collective-permute-start | bytes 491528 | tf_op jit(solution)/shard_map/ppermute | solution.py:452
  190.7 0.9 copy-done.19
  191.6 1.6 shard_map.93
  193.2 2.7 %shard_map.95 = bf16[128,4096]{1,0:T(8,128)(2,1)} custom-call(s32[4]{0:T(128)S(1)} %copy-done.27, bf16[128,1024]{1,0:T(8,128)(2,1)S(1)} %copy-done.20, bf16[128,1024]{1,0:T(8,128)(2,1)} %collective-permute-done.17.rest_1_, bf16[128,1024]{1,0:T(8,128)(2,1)} %collective-permute-done.18.rest_2_, bf16[128,1024]{1,0:T(8,128)(2,1)} %collective-permute-done.19.rest_3_), custom_call_target="tpu_custom_call" | custom-call | bytes 4194304 | tf_op jit(solution)/shard_map/pallas_call | solution.py:43
  195.9 1.0 collective-permute-done.23.rest_3_
  197.0 2.0 %shard_map.101 = bf16[8,80,1024]{2,1,0:T(8,128)(2,1)} custom-call(s32[4]{0:T(128)S(1)} %copy-done.27, bf16[8,80,128]{2,1,0:T(8,128)(2,1)S(1)} %get-tuple-element.67.rest_0_, bf16[8,80,128]{2,1,0:T(8,128)(2,1)S(1)} %collective-permute-done.21.rest_1_, bf16[8,80,128]{2,1,0:T(8,128)(2,1)S(1)} %collective-permute-done.22.rest_2_, ...), custom_call_target="tpu_custom_call" | custom-call | bytes 4194304 | tf_op jit(solution)/shard_map/pallas_call | solution.py:43
  (128 shorter events, 10.4 us)
Async XLA Ops:
  0.6 32.8 %copy-start = (s32[16,8]{0,1:T(8,128)S(1)}, s32[16,8]{0,1:T(8,128)}, u32[]{:S(2)}) copy-start(s32[16,8]{0,1:T(8,128)} %param.11) | copy-start | bytes 1540
  0.7 11.8 %copy-start.26 = (s32[4]{0:T(128)}, s32[4]{0:T(128)S(1)}, u32[]{:S(2)}) copy-start(s32[4]{0:T(128)S(1)} %get-tuple-element.82.t) | copy-start | bytes 52
  2.0 6.4 %copy-start.2 = (bf16[1,8,80,1024]{3,2,1,0:T(8,128)(2,1)S(1)}, bf16[1,8,80,1024]{3,2,1,0:T(8,128)(2,1)}, u32[]{:S(2)}) copy-start(bf16[1,8,80,1024]{3,2,1,0:T(8,128)(2,1)} %param.8) | copy-start | bytes 3932164
  2.7 12.0 %collective-permute-start.6 = (bf16[8,80,128]{2,1,0:T(8,128)(2,1)S(1)}, bf16[8,80,128]{2,1,0:T(8,128)(2,1)S(1)}, u32[]{:S(2)}, u32[]{:S(2)}) collective-permute-start(bf16[8,80,128]{2,1,0:T(8,128)(2,1)S(1)} %get-tuple-element.47), channel_id=1, source_target_pairs={{0,2},{1,3},{2,0},{3,1},{4,6},{5,7},{6,4},{7,5},{8,10},{9,11},{10,... | collective-permute-start | bytes 491528 | tf_op jit(solution)/shard_map/ppermute | solution.py:452
  4.8 11.1 %collective-permute-start.7 = (bf16[8,80,128]{2,1,0:T(8,128)(2,1)S(1)}, bf16[8,80,128]{2,1,0:T(8,128)(2,1)S(1)}, u32[]{:S(2)}, u32[]{:S(2)}) collective-permute-start(bf16[8,80,128]{2,1,0:T(8,128)(2,1)S(1)} %get-tuple-element.48), channel_id=1, source_target_pairs={{0,4},{1,5},{2,6},{3,7},{4,0},{5,1},{6,2},{7,3},{8,12},{9,13},{10,... | collective-permute-start | bytes 491528 | tf_op jit(solution)/shard_map/ppermute | solution.py:452
  8.4 9.9 %collective-permute-start.8 = (bf16[8,80,128]{2,1,0:T(8,128)(2,1)S(1)}, bf16[8,80,128]{2,1,0:T(8,128)(2,1)S(1)}, u32[]{:S(2)}, u32[]{:S(2)}) collective-permute-start(bf16[8,80,128]{2,1,0:T(8,128)(2,1)S(1)} %get-tuple-element.49), channel_id=1, source_target_pairs={{0,6},{1,7},{2,4},{3,5},{4,2},{5,3},{6,0},{7,1},{8,14},{9,15},{10,... | collective-permute-start | bytes 491528 | tf_op jit(solution)/shard_map/ppermute | solution.py:452
  10.8 3.8 %copy-start.39 = (s32[16,8]{0,1:T(8,128)S(1)}, s32[16,8]{0,1:T(8,128)}, u32[]{:S(2)}) copy-start(s32[16,8]{0,1:T(8,128)} %param.9) | copy-start | bytes 1540
  14.7 31.8 %copy-start.28 = (s32[8]{0:T(128)}, s32[8]{0:T(128)S(1)}, u32[]{:S(2)}) copy-start(s32[8]{0:T(128)S(1)} %select_reduce_fusion.t) | copy-start | bytes 100
  20.0 13.6 %copy-start.40 = (s32[16,3]{0,1:T(4,128)S(1)}, s32[16,3]{0,1:T(4,128)}, u32[]{:S(2)}) copy-start(s32[16,3]{0,1:T(4,128)} %param.10) | copy-start | bytes 580
  20.0 28.2 %all-to-all-start = ((bf16[16,4,80,128]{3,2,1,0:T(8,128)(2,1)}), bf16[16,4,80,128]{3,2,1,0:T(8,128)(2,1)S(1)}, u32[]{:S(2)}, u32[]{:S(2)}) async-start(bf16[16,4,80,128]{3,2,1,0:T(8,128)(2,1)} %shard_map.87), calls=%async_computation | async-start | bytes 2621440 | tf_op jit(solution)/shard_map/all_to_all | solution.py:485
  27.1 8.7 %collective-permute-start.10 = (bf16[8,80,128]{2,1,0:T(8,128)(2,1)S(1)}, bf16[8,80,128]{2,1,0:T(8,128)(2,1)S(1)}, u32[]{:S(2)}, u32[]{:S(2)}) collective-permute-start(bf16[8,80,128]{2,1,0:T(8,128)(2,1)S(1)} %get-tuple-element.52), channel_id=1, source_target_pairs={{0,4},{1,5},{2,6},{3,7},{4,0},{5,1},{6,2},{7,3},{8,12},{9,13},{10,... | collective-permute-start | bytes 491528 | tf_op jit(solution)/shard_map/ppermute | solution.py:452
  27.2 10.6 %collective-permute-start.11 = (bf16[8,80,128]{2,1,0:T(8,128)(2,1)}, bf16[8,80,128]{2,1,0:T(8,128)(2,1)S(1)}, u32[]{:S(2)}, u32[]{:S(2)}) collective-permute-start(bf16[8,80,128]{2,1,0:T(8,128)(2,1)} %get-tuple-element.53), channel_id=1, source_target_pairs={{0,6},{1,7},{2,4},{3,5},{4,2},{5,3},{6,0},{7,1},{8,14},{9,15},{10,... | collective-permute-start | bytes 491528 | tf_op jit(solution)/shard_map/ppermute | solution.py:452
  28.6 26.5 %collective-permute-start.3 = (bf16[128,1024]{1,0:T(8,128)(2,1)}, bf16[128,1024]{1,0:T(8,128)(2,1)S(1)}, u32[]{:S(2)}, u32[]{:S(2)}) collective-permute-start(bf16[128,1024]{1,0:T(8,128)(2,1)} %get-tuple-element.43), channel_id=1, source_target_pairs={{0,2},{1,3},{2,0},{3,1},{4,6},{5,7},{6,4},{7,5},{8,10},{9,11},{10,... | collective-permute-start | bytes 786440 | tf_op jit(solution)/shard_map/ppermute | solution.py:452
  30.7 24.4 %collective-permute-start.4 = (bf16[128,1024]{1,0:T(8,128)(2,1)}, bf16[128,1024]{1,0:T(8,128)(2,1)S(1)}, u32[]{:S(2)}, u32[]{:S(2)}) collective-permute-start(bf16[128,1024]{1,0:T(8,128)(2,1)} %get-tuple-element.44), channel_id=1, source_target_pairs={{0,4},{1,5},{2,6},{3,7},{4,0},{5,1},{6,2},{7,3},{8,12},{9,13},{10,... | collective-permute-start | bytes 786440 | tf_op jit(solution)/shard_map/ppermute | solution.py:452
  32.0 23.2 %collective-permute-start.5 = (bf16[128,1024]{1,0:T(8,128)(2,1)}, bf16[128,1024]{1,0:T(8,128)(2,1)}, u32[]{:S(2)}, u32[]{:S(2)}) collective-permute-start(bf16[128,1024]{1,0:T(8,128)(2,1)} %get-tuple-element.45), channel_id=1, source_target_pairs={{0,6},{1,7},{2,4},{3,5},{4,2},{5,3},{6,0},{7,1},{8,14},{9,15},{10,... | collective-permute-start | bytes 786440 | tf_op jit(solution)/shard_map/ppermute | solution.py:452
  35.9 10.6 %collective-permute-start.9 = (bf16[8,80,128]{2,1,0:T(8,128)(2,1)}, bf16[8,80,128]{2,1,0:T(8,128)(2,1)S(1)}, u32[]{:S(2)}, u32[]{:S(2)}) collective-permute-start(bf16[8,80,128]{2,1,0:T(8,128)(2,1)} %get-tuple-element.51), channel_id=1, source_target_pairs={{0,2},{1,3},{2,0},{3,1},{4,6},{5,7},{6,4},{7,5},{8,10},{9,11},{10,... | collective-permute-start | bytes 491528 | tf_op jit(solution)/shard_map/ppermute | solution.py:452
  36.1 12.0 %copy-start.25 = (s32[3,4]{1,0:T(4,128)}, s32[3,4]{1,0:T(4,128)S(1)}, u32[]{:S(2)}) copy-start(s32[3,4]{1,0:T(4,128)S(1)} %pad_add_fusion.rest_4_.info) | copy-start | bytes 148
  48.2 32.5 %all-to-all-start.1 = ((bf16[16,4,80,128]{3,2,1,0:T(8,128)(2,1)}), bf16[16,4,80,128]{3,2,1,0:T(8,128)(2,1)S(1)}, u32[]{:S(2)}, u32[]{:S(2)}) async-start(bf16[16,4,80,128]{3,2,1,0:T(8,128)(2,1)} %shard_map.88.rest_0_), calls=%async_computation.1 | async-start | bytes 2621440 | tf_op jit(solution)/shard_map/all_to_all | solution.py:485
  55.1 5.0 %copy-start.31 = (bf16[128,1024]{1,0:T(8,128)(2,1)S(1)}, bf16[128,1024]{1,0:T(8,128)(2,1)}, u32[]{:S(2)}) copy-start(bf16[128,1024]{1,0:T(8,128)(2,1)} %copy-done.30) | copy-start | bytes 786436
  55.9 4.9 %copy-start.15 = (bf16[8,4,80,128]{3,2,1,0:T(8,128)(2,1)}, bf16[8,4,80,128]{3,2,1,0:T(8,128)(2,1)S(1)}, u32[]{:S(2)}) copy-start(bf16[8,4,80,128]{3,2,1,0:T(8,128)(2,1)S(1)} %shard_map.89.k_mine) | copy-start | bytes 1966084
  55.9 4.9 %collective-permute-start.12 = (bf16[8,4,80,128]{3,2,1,0:T(8,128)(2,1)S(1)}, bf16[8,4,80,128]{3,2,1,0:T(8,128)(2,1)S(1)}, u32[]{:S(2)}, u32[]{:S(2)}) collective-permute-start(bf16[8,4,80,128]{3,2,1,0:T(8,128)(2,1)S(1)} %shard_map.89.k_mine), channel_id=1, source_target_pairs={{0,1},{1,0},{2,3},{3,2},{4,5},{5,4},{6,7},{7,6},{8,9},{9,8},{10,11... | collective-permute-start | bytes 1966088 | tf_op jit(solution)/shard_map/ppermute | solution.py:452
  56.1 24.6 %collective-permute-start = (bf16[128,1024]{1,0:T(8,128)(2,1)S(1)}, bf16[128,1024]{1,0:T(8,128)(2,1)S(1)}, u32[]{:S(2)}, u32[]{:S(2)}) collective-permute-start(bf16[128,1024]{1,0:T(8,128)(2,1)S(1)} %copy-done.35), channel_id=1, source_target_pairs={{0,2},{1,3},{2,0},{3,1},{4,6},{5,7},{6,4},{7,5},{8,10},{9,11},{10,... | collective-permute-start | bytes 786440 | tf_op jit(solution)/shard_map/ppermute | solution.py:452
  57.2 23.5 %collective-permute-start.1 = (bf16[128,1024]{1,0:T(8,128)(2,1)S(1)}, bf16[128,1024]{1,0:T(8,128)(2,1)S(1)}, u32[]{:S(2)}, u32[]{:S(2)}) collective-permute-start(bf16[128,1024]{1,0:T(8,128)(2,1)S(1)} %copy-done.33), channel_id=1, source_target_pairs={{0,4},{1,5},{2,6},{3,7},{4,0},{5,1},{6,2},{7,3},{8,12},{9,13},{10,... | collective-permute-start | bytes 786440 | tf_op jit(solution)/shard_map/ppermute | solution.py:452
  60.1 20.6 %collective-permute-start.2 = (bf16[128,1024]{1,0:T(8,128)(2,1)S(1)}, bf16[128,1024]{1,0:T(8,128)(2,1)S(1)}, u32[]{:S(2)}, u32[]{:S(2)}) collective-permute-start(bf16[128,1024]{1,0:T(8,128)(2,1)S(1)} %copy-done.31), channel_id=1, source_target_pairs={{0,6},{1,7},{2,4},{3,5},{4,2},{5,3},{6,0},{7,1},{8,14},{9,15},{10,... | collective-permute-start | bytes 786440 | tf_op jit(solution)/shard_map/ppermute | solution.py:452
  81.6 2.1 %collective-permute-start.13 = (bf16[8,4,80,128]{3,2,1,0:T(8,128)(2,1)S(1)}, bf16[8,4,80,128]{3,2,1,0:T(8,128)(2,1)S(1)}, u32[]{:S(2)}, u32[]{:S(2)}) collective-permute-start(bf16[8,4,80,128]{3,2,1,0:T(8,128)(2,1)S(1)} %shard_map.91.v_mine), channel_id=1, source_target_pairs={{0,1},{1,0},{2,3},{3,2},{4,5},{5,4},{6,7},{7,6},{8,9},{9,8},{10,11... | collective-permute-start | bytes 1966088 | tf_op jit(solution)/shard_map/ppermute | solution.py:452
  102.8 4.9 %collective-permute-start.24 = (bf16[8,4,80,128]{3,2,1,0:T(8,128)(2,1)}, bf16[8,4,80,128]{3,2,1,0:T(8,128)(2,1)S(1)}, u32[]{:S(2)}, u32[]{:S(2)}) collective-permute-start(bf16[8,4,80,128]{3,2,1,0:T(8,128)(2,1)} %get-tuple-element.72), channel_id=1, source_target_pairs={{0,1},{1,0},{2,3},{3,2},{4,5},{5,4},{6,7},{7,6},{8,9},{9,8},{10,11... | collective-permute-start | bytes 1966088 | tf_op jit(solution)/shard_map/ppermute | solution.py:452
  102.9 43.3 %collective-permute-start.14 = (bf16[128,1024]{1,0:T(8,128)(2,1)}, bf16[128,1024]{1,0:T(8,128)(2,1)S(1)}, u32[]{:S(2)}, u32[]{:S(2)}) collective-permute-start(bf16[128,1024]{1,0:T(8,128)(2,1)} %get-tuple-element.57.a1), channel_id=1, source_target_pairs={{0,2},{1,3},{2,0},{3,1},{4,6},{5,7},{6,4},{7,5},{8,10},{9,11},{10,... | collective-permute-start | bytes 786440 | tf_op jit(solution)/shard_map/ppermute | solution.py:452
  103.0 43.2 %collective-permute-start.15 = (bf16[128,1024]{1,0:T(8,128)(2,1)}, bf16[128,1024]{1,0:T(8,128)(2,1)S(1)}, u32[]{:S(2)}, u32[]{:S(2)}) collective-permute-start(bf16[128,1024]{1,0:T(8,128)(2,1)} %get-tuple-element.58.a2), channel_id=1, source_target_pairs={{0,4},{1,5},{2,6},{3,7},{4,0},{5,1},{6,2},{7,3},{8,12},{9,13},{10,... | collective-permute-start | bytes 786440 | tf_op jit(solution)/shard_map/ppermute | solution.py:452
  107.0 39.2 %collective-permute-start.16 = (bf16[128,1024]{1,0:T(8,128)(2,1)}, bf16[128,1024]{1,0:T(8,128)(2,1)S(1)}, u32[]{:S(2)}, u32[]{:S(2)}) collective-permute-start(bf16[128,1024]{1,0:T(8,128)(2,1)} %get-tuple-element.59.a3), channel_id=1, source_target_pairs={{0,6},{1,7},{2,4},{3,5},{4,2},{5,3},{6,0},{7,1},{8,14},{9,15},{10,... | collective-permute-start | bytes 786440 | tf_op jit(solution)/shard_map/ppermute | solution.py:452
  110.7 40.3 %all-to-all-start.3 = ((bf16[16,4,80,128]{3,2,1,0:T(8,128)(2,1)}), bf16[16,4,80,128]{3,2,1,0:T(8,128)(2,1)S(1)}, u32[]{:S(2)}, u32[]{:S(2)}) async-start(bf16[16,4,80,128]{3,2,1,0:T(8,128)(2,1)} %shard_map.99), calls=%async_computation.3 | async-start | bytes 2621440 | tf_op jit(solution)/shard_map/all_to_all | solution.py:485
  147.0 2.3 %collective-permute-start.20 = (bf16[8,4,80,128]{3,2,1,0:T(8,128)(2,1)}, bf16[8,4,80,128]{3,2,1,0:T(8,128)(2,1)S(1)}, u32[]{:S(2)}, u32[]{:S(2)}) collective-permute-start(bf16[8,4,80,128]{3,2,1,0:T(8,128)(2,1)} %shard_map.96), channel_id=1, source_target_pairs={{0,1},{1,0},{2,3},{3,2},{4,5},{5,4},{6,7},{7,6},{8,9},{9,8},{10,11... | collective-permute-start | bytes 1966088 | tf_op jit(solution)/shard_map/ppermute | solution.py:452
  151.0 14.9 %copy-start.29 = (s32[8]{0:T(128)S(1)}, s32[8]{0:T(128)}, u32[]{:S(2)}) copy-start(s32[8]{0:T(128)} %copy-done.28) | copy-start | bytes 100
  151.1 31.7 %all-to-all-start.2 = ((bf16[16,4,80,128]{3,2,1,0:T(8,128)(2,1)}), bf16[16,4,80,128]{3,2,1,0:T(8,128)(2,1)S(1)}, u32[]{:S(2)}, u32[]{:S(2)}) async-start(bf16[16,4,80,128]{3,2,1,0:T(8,128)(2,1)} %copy-done.3), calls=%async_computation.2 | async-start | bytes 2621440 | tf_op jit(solution)/shard_map/all_to_all | solution.py:485
  161.1 22.2 %collective-permute-start.17 = (bf16[128,1024]{1,0:T(8,128)(2,1)}, bf16[128,1024]{1,0:T(8,128)(2,1)}, u32[]{:S(2)}, u32[]{:S(2)}) collective-permute-start(bf16[128,1024]{1,0:T(8,128)(2,1)} %get-tuple-element.62), channel_id=1, source_target_pairs={{0,2},{1,3},{2,0},{3,1},{4,6},{5,7},{6,4},{7,5},{8,10},{9,11},{10,... | collective-permute-start | bytes 786440 | tf_op jit(solution)/shard_map/ppermute | solution.py:452
  161.2 24.7 %collective-permute-start.18 = (bf16[128,1024]{1,0:T(8,128)(2,1)}, bf16[128,1024]{1,0:T(8,128)(2,1)}, u32[]{:S(2)}, u32[]{:S(2)}) collective-permute-start(bf16[128,1024]{1,0:T(8,128)(2,1)} %get-tuple-element.63), channel_id=1, source_target_pairs={{0,4},{1,5},{2,6},{3,7},{4,0},{5,1},{6,2},{7,3},{8,12},{9,13},{10,... | collective-permute-start | bytes 786440 | tf_op jit(solution)/shard_map/ppermute | solution.py:452
  165.2 25.4 %copy-start.9 = (bf16[128,1024]{1,0:T(8,128)(2,1)S(1)}, bf16[128,1024]{1,0:T(8,128)(2,1)}, u32[]{:S(2)}) copy-start(bf16[128,1024]{1,0:T(8,128)(2,1)} %copy-done.8) | copy-start | bytes 786436
  165.2 25.5 %copy-start.11 = (bf16[128,1024]{1,0:T(8,128)(2,1)S(1)}, bf16[128,1024]{1,0:T(8,128)(2,1)}, u32[]{:S(2)}) copy-start(bf16[128,1024]{1,0:T(8,128)(2,1)} %copy-done.10) | copy-start | bytes 786436
  165.2 25.5 %copy-start.13 = (bf16[128,1024]{1,0:T(8,128)(2,1)S(1)}, bf16[128,1024]{1,0:T(8,128)(2,1)}, u32[]{:S(2)}) copy-start(bf16[128,1024]{1,0:T(8,128)(2,1)} %copy-done.12) | copy-start | bytes 786436
  165.2 25.5 %copy-start.27 = (s32[4]{0:T(128)S(1)}, s32[4]{0:T(128)}, u32[]{:S(2)}) copy-start(s32[4]{0:T(128)} %copy-done.26) | copy-start | bytes 52
  165.2 20.7 %collective-permute-start.19 = (bf16[128,1024]{1,0:T(8,128)(2,1)}, bf16[128,1024]{1,0:T(8,128)(2,1)}, u32[]{:S(2)}, u32[]{:S(2)}) collective-permute-start(bf16[128,1024]{1,0:T(8,128)(2,1)} %get-tuple-element.64), channel_id=1, source_target_pairs={{0,6},{1,7},{2,4},{3,5},{4,2},{5,3},{6,0},{7,1},{8,14},{9,15},{10,... | collective-permute-start | bytes 786440 | tf_op jit(solution)/shard_map/ppermute | solution.py:452
  168.6 14.7 %copy-start.37 = (bf16[8,80,128]{2,1,0:T(8,128)(2,1)S(1)}, bf16[8,80,128]{2,1,0:T(8,128)(2,1)}, u32[]{:S(2)}) copy-start(bf16[8,80,128]{2,1,0:T(8,128)(2,1)} %copy-done.36) | copy-start | bytes 491524
  168.6 19.5 %collective-permute-start.25 = (bf16[8,80,128]{2,1,0:T(8,128)(2,1)}, bf16[8,80,128]{2,1,0:T(8,128)(2,1)S(1)}, u32[]{:S(2)}, u32[]{:S(2)}) collective-permute-start(bf16[8,80,128]{2,1,0:T(8,128)(2,1)} %get-tuple-element.74), channel_id=1, source_target_pairs={{0,2},{1,3},{2,0},{3,1},{4,6},{5,7},{6,4},{7,5},{8,10},{9,11},{10,... | collective-permute-start | bytes 491528 | tf_op jit(solution)/shard_map/ppermute | solution.py:452
  168.6 27.3 %collective-permute-start.26 = (bf16[8,80,128]{2,1,0:T(8,128)(2,1)}, bf16[8,80,128]{2,1,0:T(8,128)(2,1)S(1)}, u32[]{:S(2)}, u32[]{:S(2)}) collective-permute-start(bf16[8,80,128]{2,1,0:T(8,128)(2,1)} %get-tuple-element.75), channel_id=1, source_target_pairs={{0,4},{1,5},{2,6},{3,7},{4,0},{5,1},{6,2},{7,3},{8,12},{9,13},{10,... | collective-permute-start | bytes 491528 | tf_op jit(solution)/shard_map/ppermute | solution.py:452
  182.7 10.5 %copy-start.20 = (bf16[128,1024]{1,0:T(8,128)(2,1)S(1)}, bf16[128,1024]{1,0:T(8,128)(2,1)}, u32[]{:S(2)}) copy-start(bf16[128,1024]{1,0:T(8,128)(2,1)} %get-tuple-element.61.rest_0_) | copy-start | bytes 786436
  183.3 12.6 %collective-permute-start.27 = (bf16[8,80,128]{2,1,0:T(8,128)(2,1)S(1)}, bf16[8,80,128]{2,1,0:T(8,128)(2,1)S(1)}, u32[]{:S(2)}, u32[]{:S(2)}) collective-permute-start(bf16[8,80,128]{2,1,0:T(8,128)(2,1)S(1)} %copy-done.37), channel_id=1, source_target_pairs={{0,6},{1,7},{2,4},{3,5},{4,2},{5,3},{6,0},{7,1},{8,14},{9,15},{10,... | collective-permute-start | bytes 491528 | tf_op jit(solution)/shard_map/ppermute | solution.py:452
  186.0 10.0 %collective-permute-start.21 = (bf16[8,80,128]{2,1,0:T(8,128)(2,1)S(1)}, bf16[8,80,128]{2,1,0:T(8,128)(2,1)S(1)}, u32[]{:S(2)}, u32[]{:S(2)}) collective-permute-start(bf16[8,80,128]{2,1,0:T(8,128)(2,1)S(1)} %get-tuple-element.68), channel_id=1, source_target_pairs={{0,2},{1,3},{2,0},{3,1},{4,6},{5,7},{6,4},{7,5},{8,10},{9,11},{10,... | collective-permute-start | bytes 491528 | tf_op jit(solution)/shard_map/ppermute | solution.py:452
  186.0 10.0 %collective-permute-start.22 = (bf16[8,80,128]{2,1,0:T(8,128)(2,1)S(1)}, bf16[8,80,128]{2,1,0:T(8,128)(2,1)S(1)}, u32[]{:S(2)}, u32[]{:S(2)}) collective-permute-start(bf16[8,80,128]{2,1,0:T(8,128)(2,1)S(1)} %get-tuple-element.69), channel_id=1, source_target_pairs={{0,4},{1,5},{2,6},{3,7},{4,0},{5,1},{6,2},{7,3},{8,12},{9,13},{10,... | collective-permute-start | bytes 491528 | tf_op jit(solution)/shard_map/ppermute | solution.py:452
  188.1 8.8 %collective-permute-start.23 = (bf16[8,80,128]{2,1,0:T(8,128)(2,1)S(1)}, bf16[8,80,128]{2,1,0:T(8,128)(2,1)S(1)}, u32[]{:S(2)}, u32[]{:S(2)}) collective-permute-start(bf16[8,80,128]{2,1,0:T(8,128)(2,1)S(1)} %get-tuple-element.70), channel_id=1, source_target_pairs={{0,6},{1,7},{2,4},{3,5},{4,2},{5,3},{6,0},{7,1},{8,14},{9,15},{10,... | collective-permute-start | bytes 491528 | tf_op jit(solution)/shard_map/ppermute | solution.py:452
  (26 other events, 30.5 us)

commit v2 on v1

--- a/solution.py
+++ b/solution.py
@@ -120,7 +120,7 @@
 def outgoing_sums(owner, own, other):
     def body(t, a, b, *rest):
         for j in range(TPS):
-            rest[-1][t[j]] = (a[j] + b[j].astype(F32)).astype(BF)
+            rest[-1][t[j]] = (a[j].astype(F32) + b[j].astype(F32)).astype(BF)
 
     return copier(body, struct(16, *PIECES[1:]), owner, own, other)
 
@@ -154,7 +154,7 @@
 
 LANES = [slice(i * HD, (i + 1) * HD) for i in range(TT // HD)]
 HEADS = [slice(h * TOK, (h + 1) * TOK) for h in range(GROUP)]
-CH_S, CH_O, CH_D = 256, 512, 512
+CH_S, CH_O, CH_D = 128, 512, 512
 
 
 def cuts(size):
@@ -185,7 +185,7 @@
 
             @pl.when(core == p)
             def _():
-                mine[j] = halves[p]
+                mine[j] = halves[p].astype(BF)
                 other[j] = halves[1 - p].astype(BF)
 
 
@@ -386,7 +386,7 @@
 TEXT_OUT = (struct(TOK, QW),) * 4
 TEXT_KEPT = (kept((TOK, QW)),) * 4
 TILES = [fixed(PIECES)] * 2
-TILES_OUT = (jax.ShapeDtypeStruct(PIECES, F32), struct(*PIECES))
+TILES_OUT = (struct(*PIECES),) * 2
 TILES_KEPT = (kept(PIECES),) * 2
 TILE_ROWS, TILE_COLUMNS = (TPS, TT, HD), (TPS, HD, TT)
 

time: 201 us -> 206 us (1.025); the launches traced: 199 us -> 206 us
  Pallas kernels: 76.7 us -> 81.6 us
  waiting for transfers between devices: 31.1 us -> 35 us
    ppermute x28, waiting for transfers between devices: 21 us -> 23.6 us  [swap(): return lax.ppermute(x, 'seq', [(i, i ^ mask) for i in range(N_SEQ)])]
  transfers between devices with their start and end apart: 32 -> 32, of which waited for: 9 -> 8; matrix products, arithmetic and copies ran while one was open for 1% -> 1% of each run, Pallas kernels for 27% -> 28%
where the time goes in v2:
time: 206 us
  Pallas kernels  81.6 us (40%)
  starting transfers between devices  73.7 us (36%)
  waiting for transfers between devices  35 us (17%)
  local copies, waits for them, and re-layouts  14.1 us (7%)
    ppermute x28, starting transfers between devices, swap(): return lax.ppermute(x, 'seq', [(i, i ^ mask) for i in range(N_SEQ)])  38.1 us
    all_to_all x4, starting transfers between devices, exchange(): return lax.all_to_all(x, 'dp', split_axis=0, concat_axis=0, tiled=True)  35.6 us
    pallas_call x1, Pallas kernels, gradients(): attention_call(grads_body, 60, TEXT_OUT + TILES_OUT, TEXT + [by_block(*E_...  23.8 us
    ppermute x28, waiting for transfers between devices, swap(): return lax.ppermute(x, 'seq', [(i, i ^ mask) for i in range(N_SEQ)])  23.6 us
    pallas_call x1, Pallas kernels, weights(): attention_call(weights_body, 0, (struct(CHIPS, *E_SHAPE), jax.ShapeDtypeS...  21 us
    pallas_call x1, Pallas kernels, outputs(): attention_call(outputs_body, 40, TEXT_OUT + (struct(CHIPS, *D_SHAPE),) +...  19.4 us
    pallas_call x11, Pallas kernels, copier(): pl.pallas_call(body, out_shape=shapes, grid_spec=pltpu.PrefetchScalarGrid...  15.1 us
    unnamed x84, local copies, waits for them, and re-layouts  13.6 us
  transfers between devices with their start and end apart: 32, of which 8 were waited for; matrix products, arithmetic and copies ran while one was open for 1% of the time, Pallas kernels for 28%

profile of v2, /device:TPU:0, one launch (start us, length us, event | category | flops | bytes accessed | tf_op | source)
XLA Modules:
  0.0 206.3 jit_solution(8228759041464402765)
XLA Ops:
  0.7 1.3 copy-done.1
  2.7 2.1 %collective-permute-start.6 = (bf16[8,80,128]{2,1,0:T(8,128)(2,1)S(1)}, bf16[8,80,128]{2,1,0:T(8,128)(2,1)S(1)}, u32[]{:S(2)}, u32[]{:S(2)}) collective-permute-start(bf16[8,80,128]{2,1,0:T(8,128)(2,1)S(1)} %get-tuple-element.47), channel_id=1, source_target_pairs={{0,2},{1,3},{2,0},{3,1},{4,6},{5,7},{6,4},{7,5},{8,10},{9,11},{10,... | collective-permute-start | bytes 491528 | tf_op jit(solution)/shard_map/ppermute | solution.py:452
  4.8 3.6 %collective-permute-start.7 = (bf16[8,80,128]{2,1,0:T(8,128)(2,1)S(1)}, bf16[8,80,128]{2,1,0:T(8,128)(2,1)S(1)}, u32[]{:S(2)}, u32[]{:S(2)}) collective-permute-start(bf16[8,80,128]{2,1,0:T(8,128)(2,1)S(1)} %get-tuple-element.48), channel_id=1, source_target_pairs={{0,4},{1,5},{2,6},{3,7},{4,0},{5,1},{6,2},{7,3},{8,12},{9,13},{10,... | collective-permute-start | bytes 491528 | tf_op jit(solution)/shard_map/ppermute | solution.py:452
  8.4 1.2 copy-done.4
  9.6 1.2 copy-done.5
  10.8 1.6 shard_map.85
  12.5 0.7 copy-done.30
  13.2 0.7 copy-done.32
  13.9 0.7 copy-done.34
  14.7 1.2 collective-permute-done.7.rest_2_
  15.9 2.4 %collective-permute-done.8.rest_3_ = bf16[8,80,128]{2,1,0:T(8,128)(2,1)S(1)} collective-permute-done((bf16[8,80,128]{2,1,0:T(8,128)(2,1)S(1)}, bf16[8,80,128]{2,1,0:T(8,128)(2,1)S(1)}, u32[]{:S(2)}, u32[]{:S(2)}) %collective-permute-start.8) | collective-permute-done | bytes 163872 | tf_op jit(solution)/shard_map/ppermute | solution.py:452
  18.3 1.6 shard_map.87
  20.0 7.2 %all-to-all-start = ((bf16[16,4,80,128]{3,2,1,0:T(8,128)(2,1)}), bf16[16,4,80,128]{3,2,1,0:T(8,128)(2,1)S(1)}, u32[]{:S(2)}, u32[]{:S(2)}) async-start(bf16[16,4,80,128]{3,2,1,0:T(8,128)(2,1)} %shard_map.87), calls=%async_computation | async-start | bytes 2621440 | tf_op jit(solution)/shard_map/all_to_all | solution.py:485
  27.2 1.5 collective-permute-start.10
  29.2 4.1 %collective-permute-start.4 = (bf16[128,1024]{1,0:T(8,128)(2,1)}, bf16[128,1024]{1,0:T(8,128)(2,1)S(1)}, u32[]{:S(2)}, u32[]{:S(2)}) collective-permute-start(bf16[128,1024]{1,0:T(8,128)(2,1)} %get-tuple-element.44), channel_id=1, source_target_pairs={{0,4},{1,5},{2,6},{3,7},{4,0},{5,1},{6,2},{7,3},{8,12},{9,13},{10,... | collective-permute-start | bytes 786440 | tf_op jit(solution)/shard_map/ppermute | solution.py:452
  34.4 3.2 %collective-permute-start.11 = (bf16[8,80,128]{2,1,0:T(8,128)(2,1)}, bf16[8,80,128]{2,1,0:T(8,128)(2,1)S(1)}, u32[]{:S(2)}, u32[]{:S(2)}) collective-permute-start(bf16[8,80,128]{2,1,0:T(8,128)(2,1)} %get-tuple-element.53), channel_id=1, source_target_pairs={{0,6},{1,7},{2,4},{3,5},{4,2},{5,3},{6,0},{7,1},{8,14},{9,15},{10,... | collective-permute-start | bytes 491528 | tf_op jit(solution)/shard_map/ppermute | solution.py:452
  37.9 13.2 %collective-permute-done.11.rest_3_ = bf16[8,80,128]{2,1,0:T(8,128)(2,1)S(1)} collective-permute-done((bf16[8,80,128]{2,1,0:T(8,128)(2,1)}, bf16[8,80,128]{2,1,0:T(8,128)(2,1)S(1)}, u32[]{:S(2)}, u32[]{:S(2)}) %collective-permute-start.11) | collective-permute-done | bytes 163872 | tf_op jit(solution)/shard_map/ppermute | solution.py:452
  51.0 1.7 shard_map.88.rest_0_
  52.7 7.0 %all-to-all-start.1 = ((bf16[16,4,80,128]{3,2,1,0:T(8,128)(2,1)}), bf16[16,4,80,128]{3,2,1,0:T(8,128)(2,1)S(1)}, u32[]{:S(2)}, u32[]{:S(2)}) async-start(bf16[16,4,80,128]{3,2,1,0:T(8,128)(2,1)} %shard_map.88.rest_0_), calls=%async_computation.1 | async-start | bytes 2621440 | tf_op jit(solution)/shard_map/all_to_all | solution.py:485
  60.9 2.5 %collective-permute-start.1 = (bf16[128,1024]{1,0:T(8,128)(2,1)S(1)}, bf16[128,1024]{1,0:T(8,128)(2,1)S(1)}, u32[]{:S(2)}, u32[]{:S(2)}) collective-permute-start(bf16[128,1024]{1,0:T(8,128)(2,1)S(1)} %copy-done.33), channel_id=1, source_target_pairs={{0,4},{1,5},{2,6},{3,7},{4,0},{5,1},{6,2},{7,3},{8,12},{9,13},{10,... | collective-permute-start | bytes 786440 | tf_op jit(solution)/shard_map/ppermute | solution.py:452
  63.4 2.0 collective-permute-start.2
  65.4 0.8 copy-done.38
  66.3 21.0 %shard_map.90 = (bf16[4,4,1024,640]{3,2,1,0:T(8,128)(2,1)}, f32[4,1024,128]{2,1,0:T(8,128)}) custom-call(s32[3,4]{1,0:T(4,128)} %copy-done.25, bf16[128,4096]{1,0:T(8,128)(2,1)} %bitcast.14, bf16[128,1024]{1,0:T(8,128)(2,1)} %copy-done.21, bf16[128,1024]{1,0:T(8,128)(2,1)} %copy-done.22, bf16[128,1024]{1,0:T(8,128)(2,1)} %collective-permute-done.5.rest_3_.q3, ...), custom_call_target="tpu_custom_call" | custom-call | tf_op jit(solution)/shard_map/pallas_call | solution.py:395
  88.2 2.1 %collective-permute-done.13.v_other = bf16[8,4,80,128]{3,2,1,0:T(8,128)(2,1)S(1)} collective-permute-done((bf16[8,4,80,128]{3,2,1,0:T(8,128)(2,1)S(1)}, bf16[8,4,80,128]{3,2,1,0:T(8,128)(2,1)S(1)}, u32[]{:S(2)}, u32[]{:S(2)}) %collective-permute-start.13) | collective-permute-done | bytes 655392 | tf_op jit(solution)/shard_map/ppermute | solution.py:452
  90.3 0.8 copy-done.41
  91.1 19.4 %shard_map.92 = (bf16[128,1024]{1,0:T(8,128)(2,1)}, bf16[128,1024]{1,0:T(8,128)(2,1)}, bf16[128,1024]{1,0:T(8,128)(2,1)}, bf16[128,1024]{1,0:T(8,128)(2,1)}, bf1...) custom-call(s32[3,4]{1,0:T(4,128)} %copy-done.25, ...), custom_call_target="tpu_custom_call" | custom-call | flops 40000000000 | bytes 41943040 | tf_op jit(solution)/shard_map/pallas_call | solution.py:414
  110.7 2.7 %collective-permute-start.15 = (bf16[128,1024]{1,0:T(8,128)(2,1)}, bf16[128,1024]{1,0:T(8,128)(2,1)S(1)}, u32[]{:S(2)}, u32[]{:S(2)}) collective-permute-start(bf16[128,1024]{1,0:T(8,128)(2,1)} %get-tuple-element.58.a2), channel_id=1, source_target_pairs={{0,4},{1,5},{2,6},{3,7},{4,0},{5,1},{6,2},{7,3},{8,12},{9,13},{10,... | collective-permute-start | bytes 786440 | tf_op jit(solution)/shard_map/ppermute | solution.py:452
  113.4 2.0 collective-permute-start.16
  115.4 1.1 copy-done.15
  116.5 1.8 shard_map.99
  118.2 11.6 %all-to-all-start.3 = ((bf16[16,4,80,128]{3,2,1,0:T(8,128)(2,1)}), bf16[16,4,80,128]{3,2,1,0:T(8,128)(2,1)S(1)}, u32[]{:S(2)}, u32[]{:S(2)}) async-start(bf16[16,4,80,128]{3,2,1,0:T(8,128)(2,1)} %shard_map.99), calls=%async_computation.3 | async-start | bytes 2621440 | tf_op jit(solution)/shard_map/all_to_all | solution.py:485
  129.9 23.8 %shard_map.94 = (bf16[128,1024]{1,0:T(8,128)(2,1)}, bf16[128,1024]{1,0:T(8,128)(2,1)}, bf16[128,1024]{1,0:T(8,128)(2,1)}, bf16[128,1024]{1,0:T(8,128)(2,1)}, bf1...) custom-call(s32[3,4]{1,0:T(4,128)} %copy-done.25, bf16[128,4096]{1,0:T(8,128)(2,1)} %bitcast.15, ...), custom_call_target="tpu_custom_call" | custom-call | flops 60000002048 | bytes 62914560 | tf_op jit(solution)/shard_map/pallas_call | solution.py:430
  154.6 2.3 %collective-permute-done.20.b = bf16[8,4,80,128]{3,2,1,0:T(8,128)(2,1)S(1)} collective-permute-done((bf16[8,4,80,128]{3,2,1,0:T(8,128)(2,1)}, bf16[8,4,80,128]{3,2,1,0:T(8,128)(2,1)S(1)}, u32[]{:S(2)}, u32[]{:S(2)}) %collective-permute-start.20) | collective-permute-done | bytes 655392 | tf_op jit(solution)/shard_map/ppermute | solution.py:452
  157.6 1.0 copy-done.3
  158.7 9.8 %all-to-all-start.2 = ((bf16[16,4,80,128]{3,2,1,0:T(8,128)(2,1)}), bf16[16,4,80,128]{3,2,1,0:T(8,128)(2,1)S(1)}, u32[]{:S(2)}, u32[]{:S(2)}) async-start(bf16[16,4,80,128]{3,2,1,0:T(8,128)(2,1)} %copy-done.3), calls=%async_computation.2 | async-start | bytes 2621440 | tf_op jit(solution)/shard_map/all_to_all | solution.py:485
  168.5 2.7 %collective-permute-start.18 = (bf16[128,1024]{1,0:T(8,128)(2,1)}, bf16[128,1024]{1,0:T(8,128)(2,1)}, u32[]{:S(2)}, u32[]{:S(2)}) collective-permute-start(bf16[128,1024]{1,0:T(8,128)(2,1)} %get-tuple-element.63), channel_id=1, source_target_pairs={{0,4},{1,5},{2,6},{3,7},{4,0},{5,1},{6,2},{7,3},{8,12},{9,13},{10,... | collective-permute-start | bytes 786440 | tf_op jit(solution)/shard_map/ppermute | solution.py:452
  171.2 2.1 %collective-permute-start.19 = (bf16[128,1024]{1,0:T(8,128)(2,1)}, bf16[128,1024]{1,0:T(8,128)(2,1)}, u32[]{:S(2)}, u32[]{:S(2)}) collective-permute-start(bf16[128,1024]{1,0:T(8,128)(2,1)} %get-tuple-element.64), channel_id=1, source_target_pairs={{0,6},{1,7},{2,4},{3,5},{4,2},{5,3},{6,0},{7,1},{8,14},{9,15},{10,... | collective-permute-start | bytes 786440 | tf_op jit(solution)/shard_map/ppermute | solution.py:452
  173.3 1.3 shard_map.100
  175.9 2.7 %collective-permute-start.26 = (bf16[8,80,128]{2,1,0:T(8,128)(2,1)}, bf16[8,80,128]{2,1,0:T(8,128)(2,1)S(1)}, u32[]{:S(2)}, u32[]{:S(2)}) collective-permute-start(bf16[8,80,128]{2,1,0:T(8,128)(2,1)} %get-tuple-element.75), channel_id=1, source_target_pairs={{0,4},{1,5},{2,6},{3,7},{4,0},{5,1},{6,2},{7,3},{8,12},{9,13},{10,... | collective-permute-start | bytes 491528 | tf_op jit(solution)/shard_map/ppermute | solution.py:452
  178.6 11.4 %all-to-all-done.2.s = bf16[16,4,80,128]{3,2,1,0:T(8,128)(2,1)S(1)} async-done(((bf16[16,4,80,128]{3,2,1,0:T(8,128)(2,1)}), bf16[16,4,80,128]{3,2,1,0:T(8,128)(2,1)S(1)}, u32[]{:S(2)}, u32[]{:S(2)}) %all-to-all-start.2) | async-done | bytes 1310752 | tf_op jit(solution)/shard_map/all_to_all | solution.py:485
  190.6 1.3 collective-permute-start.27
  192.0 3.4 %collective-permute-start.22 = (bf16[8,80,128]{2,1,0:T(8,128)(2,1)S(1)}, bf16[8,80,128]{2,1,0:T(8,128)(2,1)S(1)}, u32[]{:S(2)}, u32[]{:S(2)}) collective-permute-start(bf16[8,80,128]{2,1,0:T(8,128)(2,1)S(1)} %get-tuple-element.69), channel_id=1, source_target_pairs={{0,4},{1,5},{2,6},{3,7},{4,0},{5,1},{6,2},{7,3},{8,12},{9,13},{10,... | collective-permute-start | bytes 491528 | tf_op jit(solution)/shard_map/ppermute | solution.py:452
  195.4 1.2 collective-permute-start.23
  196.7 0.9 copy-done.19
  197.6 1.6 shard_map.93
  199.2 2.7 %shard_map.95 = bf16[128,4096]{1,0:T(8,128)(2,1)} custom-call(s32[4]{0:T(128)S(1)} %copy-done.27, bf16[128,1024]{1,0:T(8,128)(2,1)S(1)} %copy-done.20, bf16[128,1024]{1,0:T(8,128)(2,1)} %collective-permute-done.17.rest_1_, bf16[128,1024]{1,0:T(8,128)(2,1)} %collective-permute-done.18.rest_2_, bf16[128,1024]{1,0:T(8,128)(2,1)} %collective-permute-done.19.rest_3_), custom_call_target="tpu_custom_call" | custom-call | bytes 4194304 | tf_op jit(solution)/shard_map/pallas_call | solution.py:43
  202.0 2.3 %collective-permute-done.23.rest_3_ = bf16[8,80,128]{2,1,0:T(8,128)(2,1)S(1)} collective-permute-done((bf16[8,80,128]{2,1,0:T(8,128)(2,1)S(1)}, bf16[8,80,128]{2,1,0:T(8,128)(2,1)S(1)}, u32[]{:S(2)}, u32[]{:S(2)}) %collective-permute-start.23) | collective-permute-done | bytes 163872 | tf_op jit(solution)/shard_map/ppermute | solution.py:452
  204.3 2.0 shard_map.101
  (128 shorter events, 8.5 us)
Async XLA Ops:
  0.6 32.8 %copy-start = (s32[16,8]{0,1:T(8,128)S(1)}, s32[16,8]{0,1:T(8,128)}, u32[]{:S(2)}) copy-start(s32[16,8]{0,1:T(8,128)} %param.11) | copy-start | bytes 1540
  0.7 11.8 %copy-start.26 = (s32[4]{0:T(128)}, s32[4]{0:T(128)S(1)}, u32[]{:S(2)}) copy-start(s32[4]{0:T(128)S(1)} %get-tuple-element.82.t) | copy-start | bytes 52
  2.0 6.4 %copy-start.2 = (bf16[1,8,80,1024]{3,2,1,0:T(8,128)(2,1)S(1)}, bf16[1,8,80,1024]{3,2,1,0:T(8,128)(2,1)}, u32[]{:S(2)}) copy-start(bf16[1,8,80,1024]{3,2,1,0:T(8,128)(2,1)} %param.8) | copy-start | bytes 3932164
  2.7 12.0 %collective-permute-start.6 = (bf16[8,80,128]{2,1,0:T(8,128)(2,1)S(1)}, bf16[8,80,128]{2,1,0:T(8,128)(2,1)S(1)}, u32[]{:S(2)}, u32[]{:S(2)}) collective-permute-start(bf16[8,80,128]{2,1,0:T(8,128)(2,1)S(1)} %get-tuple-element.47), channel_id=1, source_target_pairs={{0,2},{1,3},{2,0},{3,1},{4,6},{5,7},{6,4},{7,5},{8,10},{9,11},{10,... | collective-permute-start | bytes 491528 | tf_op jit(solution)/shard_map/ppermute | solution.py:452
  4.8 11.1 %collective-permute-start.7 = (bf16[8,80,128]{2,1,0:T(8,128)(2,1)S(1)}, bf16[8,80,128]{2,1,0:T(8,128)(2,1)S(1)}, u32[]{:S(2)}, u32[]{:S(2)}) collective-permute-start(bf16[8,80,128]{2,1,0:T(8,128)(2,1)S(1)} %get-tuple-element.48), channel_id=1, source_target_pairs={{0,4},{1,5},{2,6},{3,7},{4,0},{5,1},{6,2},{7,3},{8,12},{9,13},{10,... | collective-permute-start | bytes 491528 | tf_op jit(solution)/shard_map/ppermute | solution.py:452
  8.4 9.9 %collective-permute-start.8 = (bf16[8,80,128]{2,1,0:T(8,128)(2,1)S(1)}, bf16[8,80,128]{2,1,0:T(8,128)(2,1)S(1)}, u32[]{:S(2)}, u32[]{:S(2)}) collective-permute-start(bf16[8,80,128]{2,1,0:T(8,128)(2,1)S(1)} %get-tuple-element.49), channel_id=1, source_target_pairs={{0,6},{1,7},{2,4},{3,5},{4,2},{5,3},{6,0},{7,1},{8,14},{9,15},{10,... | collective-permute-start | bytes 491528 | tf_op jit(solution)/shard_map/ppermute | solution.py:452
  10.8 3.8 %copy-start.39 = (s32[16,8]{0,1:T(8,128)S(1)}, s32[16,8]{0,1:T(8,128)}, u32[]{:S(2)}) copy-start(s32[16,8]{0,1:T(8,128)} %param.9) | copy-start | bytes 1540
  14.7 36.3 %copy-start.28 = (s32[8]{0:T(128)}, s32[8]{0:T(128)S(1)}, u32[]{:S(2)}) copy-start(s32[8]{0:T(128)S(1)} %select_reduce_fusion.t) | copy-start | bytes 100
  20.0 13.7 %copy-start.40 = (s32[16,3]{0,1:T(4,128)S(1)}, s32[16,3]{0,1:T(4,128)}, u32[]{:S(2)}) copy-start(s32[16,3]{0,1:T(4,128)} %param.10) | copy-start | bytes 580
  20.0 32.8 %all-to-all-start = ((bf16[16,4,80,128]{3,2,1,0:T(8,128)(2,1)}), bf16[16,4,80,128]{3,2,1,0:T(8,128)(2,1)S(1)}, u32[]{:S(2)}, u32[]{:S(2)}) async-start(bf16[16,4,80,128]{3,2,1,0:T(8,128)(2,1)} %shard_map.87), calls=%async_computation | async-start | bytes 2621440 | tf_op jit(solution)/shard_map/all_to_all | solution.py:485
  27.1 7.2 %collective-permute-start.9 = (bf16[8,80,128]{2,1,0:T(8,128)(2,1)S(1)}, bf16[8,80,128]{2,1,0:T(8,128)(2,1)S(1)}, u32[]{:S(2)}, u32[]{:S(2)}) collective-permute-start(bf16[8,80,128]{2,1,0:T(8,128)(2,1)S(1)} %get-tuple-element.51), channel_id=1, source_target_pairs={{0,2},{1,3},{2,0},{3,1},{4,6},{5,7},{6,4},{7,5},{8,10},{9,11},{10,... | collective-permute-start | bytes 491528 | tf_op jit(solution)/shard_map/ppermute | solution.py:452
  27.2 10.6 %collective-permute-start.10 = (bf16[8,80,128]{2,1,0:T(8,128)(2,1)}, bf16[8,80,128]{2,1,0:T(8,128)(2,1)S(1)}, u32[]{:S(2)}, u32[]{:S(2)}) collective-permute-start(bf16[8,80,128]{2,1,0:T(8,128)(2,1)} %get-tuple-element.52), channel_id=1, source_target_pairs={{0,4},{1,5},{2,6},{3,7},{4,0},{5,1},{6,2},{7,3},{8,12},{9,13},{10,... | collective-permute-start | bytes 491528 | tf_op jit(solution)/shard_map/ppermute | solution.py:452
  28.8 31.0 %collective-permute-start.3 = (bf16[128,1024]{1,0:T(8,128)(2,1)}, bf16[128,1024]{1,0:T(8,128)(2,1)S(1)}, u32[]{:S(2)}, u32[]{:S(2)}) collective-permute-start(bf16[128,1024]{1,0:T(8,128)(2,1)} %get-tuple-element.43), channel_id=1, source_target_pairs={{0,2},{1,3},{2,0},{3,1},{4,6},{5,7},{6,4},{7,5},{8,10},{9,11},{10,... | collective-permute-start | bytes 786440 | tf_op jit(solution)/shard_map/ppermute | solution.py:452
  29.2 30.5 %collective-permute-start.4 = (bf16[128,1024]{1,0:T(8,128)(2,1)}, bf16[128,1024]{1,0:T(8,128)(2,1)S(1)}, u32[]{:S(2)}, u32[]{:S(2)}) collective-permute-start(bf16[128,1024]{1,0:T(8,128)(2,1)} %get-tuple-element.44), channel_id=1, source_target_pairs={{0,4},{1,5},{2,6},{3,7},{4,0},{5,1},{6,2},{7,3},{8,12},{9,13},{10,... | collective-permute-start | bytes 786440 | tf_op jit(solution)/shard_map/ppermute | solution.py:452
  33.4 26.4 %collective-permute-start.5 = (bf16[128,1024]{1,0:T(8,128)(2,1)}, bf16[128,1024]{1,0:T(8,128)(2,1)}, u32[]{:S(2)}, u32[]{:S(2)}) collective-permute-start(bf16[128,1024]{1,0:T(8,128)(2,1)} %get-tuple-element.45), channel_id=1, source_target_pairs={{0,6},{1,7},{2,4},{3,5},{4,2},{5,3},{6,0},{7,1},{8,14},{9,15},{10,... | collective-permute-start | bytes 786440 | tf_op jit(solution)/shard_map/ppermute | solution.py:452
  34.4 16.7 %collective-permute-start.11 = (bf16[8,80,128]{2,1,0:T(8,128)(2,1)}, bf16[8,80,128]{2,1,0:T(8,128)(2,1)S(1)}, u32[]{:S(2)}, u32[]{:S(2)}) collective-permute-start(bf16[8,80,128]{2,1,0:T(8,128)(2,1)} %get-tuple-element.53), channel_id=1, source_target_pairs={{0,6},{1,7},{2,4},{3,5},{4,2},{5,3},{6,0},{7,1},{8,14},{9,15},{10,... | collective-permute-start | bytes 491528 | tf_op jit(solution)/shard_map/ppermute | solution.py:452
  37.8 14.9 %copy-start.25 = (s32[3,4]{1,0:T(4,128)}, s32[3,4]{1,0:T(4,128)S(1)}, u32[]{:S(2)}) copy-start(s32[3,4]{1,0:T(4,128)S(1)} %pad_add_fusion.rest_4_.info) | copy-start | bytes 148
  52.7 34.6 %all-to-all-start.1 = ((bf16[16,4,80,128]{3,2,1,0:T(8,128)(2,1)}), bf16[16,4,80,128]{3,2,1,0:T(8,128)(2,1)S(1)}, u32[]{:S(2)}, u32[]{:S(2)}) async-start(bf16[16,4,80,128]{3,2,1,0:T(8,128)(2,1)} %shard_map.88.rest_0_), calls=%async_computation.1 | async-start | bytes 2621440 | tf_op jit(solution)/shard_map/all_to_all | solution.py:485
  60.6 4.9 %copy-start.13 = (bf16[8,4,80,128]{3,2,1,0:T(8,128)(2,1)}, bf16[8,4,80,128]{3,2,1,0:T(8,128)(2,1)S(1)}, u32[]{:S(2)}) copy-start(bf16[8,4,80,128]{3,2,1,0:T(8,128)(2,1)S(1)} %shard_map.89.k_mine) | copy-start | bytes 1966084
  60.6 4.9 %collective-permute-start.12 = (bf16[8,4,80,128]{3,2,1,0:T(8,128)(2,1)S(1)}, bf16[8,4,80,128]{3,2,1,0:T(8,128)(2,1)S(1)}, u32[]{:S(2)}, u32[]{:S(2)}) collective-permute-start(bf16[8,4,80,128]{3,2,1,0:T(8,128)(2,1)S(1)} %shard_map.89.k_mine), channel_id=1, source_target_pairs={{0,1},{1,0},{2,3},{3,2},{4,5},{5,4},{6,7},{7,6},{8,9},{9,8},{10,11... | collective-permute-start | bytes 1966088 | tf_op jit(solution)/shard_map/ppermute | solution.py:452
  60.7 26.6 %collective-permute-start = (bf16[128,1024]{1,0:T(8,128)(2,1)S(1)}, bf16[128,1024]{1,0:T(8,128)(2,1)S(1)}, u32[]{:S(2)}, u32[]{:S(2)}) collective-permute-start(bf16[128,1024]{1,0:T(8,128)(2,1)S(1)} %copy-done.35), channel_id=1, source_target_pairs={{0,2},{1,3},{2,0},{3,1},{4,6},{5,7},{6,4},{7,5},{8,10},{9,11},{10,... | collective-permute-start | bytes 786440 | tf_op jit(solution)/shard_map/ppermute | solution.py:452
  60.9 26.4 %collective-permute-start.1 = (bf16[128,1024]{1,0:T(8,128)(2,1)S(1)}, bf16[128,1024]{1,0:T(8,128)(2,1)S(1)}, u32[]{:S(2)}, u32[]{:S(2)}) collective-permute-start(bf16[128,1024]{1,0:T(8,128)(2,1)S(1)} %copy-done.33), channel_id=1, source_target_pairs={{0,4},{1,5},{2,6},{3,7},{4,0},{5,1},{6,2},{7,3},{8,12},{9,13},{10,... | collective-permute-start | bytes 786440 | tf_op jit(solution)/shard_map/ppermute | solution.py:452
  63.4 23.9 %collective-permute-start.2 = (bf16[128,1024]{1,0:T(8,128)(2,1)S(1)}, bf16[128,1024]{1,0:T(8,128)(2,1)S(1)}, u32[]{:S(2)}, u32[]{:S(2)}) collective-permute-start(bf16[128,1024]{1,0:T(8,128)(2,1)S(1)} %copy-done.31), channel_id=1, source_target_pairs={{0,6},{1,7},{2,4},{3,5},{4,2},{5,3},{6,0},{7,1},{8,14},{9,15},{10,... | collective-permute-start | bytes 786440 | tf_op jit(solution)/shard_map/ppermute | solution.py:452
  88.2 2.1 %collective-permute-start.13 = (bf16[8,4,80,128]{3,2,1,0:T(8,128)(2,1)S(1)}, bf16[8,4,80,128]{3,2,1,0:T(8,128)(2,1)S(1)}, u32[]{:S(2)}, u32[]{:S(2)}) collective-permute-start(bf16[8,4,80,128]{3,2,1,0:T(8,128)(2,1)S(1)} %shard_map.91.v_mine), channel_id=1, source_target_pairs={{0,1},{1,0},{2,3},{3,2},{4,5},{5,4},{6,7},{7,6},{8,9},{9,8},{10,11... | collective-permute-start | bytes 1966088 | tf_op jit(solution)/shard_map/ppermute | solution.py:452
  110.5 4.9 %collective-permute-start.24 = (bf16[8,4,80,128]{3,2,1,0:T(8,128)(2,1)}, bf16[8,4,80,128]{3,2,1,0:T(8,128)(2,1)S(1)}, u32[]{:S(2)}, u32[]{:S(2)}) collective-permute-start(bf16[8,4,80,128]{3,2,1,0:T(8,128)(2,1)} %get-tuple-element.72), channel_id=1, source_target_pairs={{0,1},{1,0},{2,3},{3,2},{4,5},{5,4},{6,7},{7,6},{8,9},{9,8},{10,11... | collective-permute-start | bytes 1966088 | tf_op jit(solution)/shard_map/ppermute | solution.py:452
  110.6 43.1 %collective-permute-start.14 = (bf16[128,1024]{1,0:T(8,128)(2,1)}, bf16[128,1024]{1,0:T(8,128)(2,1)S(1)}, u32[]{:S(2)}, u32[]{:S(2)}) collective-permute-start(bf16[128,1024]{1,0:T(8,128)(2,1)} %get-tuple-element.57.a1), channel_id=1, source_target_pairs={{0,2},{1,3},{2,0},{3,1},{4,6},{5,7},{6,4},{7,5},{8,10},{9,11},{10,... | collective-permute-start | bytes 786440 | tf_op jit(solution)/shard_map/ppermute | solution.py:452
  110.7 43.0 %collective-permute-start.15 = (bf16[128,1024]{1,0:T(8,128)(2,1)}, bf16[128,1024]{1,0:T(8,128)(2,1)S(1)}, u32[]{:S(2)}, u32[]{:S(2)}) collective-permute-start(bf16[128,1024]{1,0:T(8,128)(2,1)} %get-tuple-element.58.a2), channel_id=1, source_target_pairs={{0,4},{1,5},{2,6},{3,7},{4,0},{5,1},{6,2},{7,3},{8,12},{9,13},{10,... | collective-permute-start | bytes 786440 | tf_op jit(solution)/shard_map/ppermute | solution.py:452
  113.4 40.3 %collective-permute-start.16 = (bf16[128,1024]{1,0:T(8,128)(2,1)}, bf16[128,1024]{1,0:T(8,128)(2,1)S(1)}, u32[]{:S(2)}, u32[]{:S(2)}) collective-permute-start(bf16[128,1024]{1,0:T(8,128)(2,1)} %get-tuple-element.59.a3), channel_id=1, source_target_pairs={{0,6},{1,7},{2,4},{3,5},{4,2},{5,3},{6,0},{7,1},{8,14},{9,15},{10,... | collective-permute-start | bytes 786440 | tf_op jit(solution)/shard_map/ppermute | solution.py:452
  118.2 40.4 %all-to-all-start.3 = ((bf16[16,4,80,128]{3,2,1,0:T(8,128)(2,1)}), bf16[16,4,80,128]{3,2,1,0:T(8,128)(2,1)S(1)}, u32[]{:S(2)}, u32[]{:S(2)}) async-start(bf16[16,4,80,128]{3,2,1,0:T(8,128)(2,1)} %shard_map.99), calls=%async_computation.3 | async-start | bytes 2621440 | tf_op jit(solution)/shard_map/all_to_all | solution.py:485
  154.6 2.3 %collective-permute-start.20 = (bf16[8,4,80,128]{3,2,1,0:T(8,128)(2,1)}, bf16[8,4,80,128]{3,2,1,0:T(8,128)(2,1)S(1)}, u32[]{:S(2)}, u32[]{:S(2)}) collective-permute-start(bf16[8,4,80,128]{3,2,1,0:T(8,128)(2,1)} %shard_map.96), channel_id=1, source_target_pairs={{0,1},{1,0},{2,3},{3,2},{4,5},{5,4},{6,7},{7,6},{8,9},{9,8},{10,11... | collective-permute-start | bytes 1966088 | tf_op jit(solution)/shard_map/ppermute | solution.py:452
  158.6 14.7 %copy-start.29 = (s32[8]{0:T(128)S(1)}, s32[8]{0:T(128)}, u32[]{:S(2)}) copy-start(s32[8]{0:T(128)} %copy-done.28) | copy-start | bytes 100
  158.7 31.4 %all-to-all-start.2 = ((bf16[16,4,80,128]{3,2,1,0:T(8,128)(2,1)}), bf16[16,4,80,128]{3,2,1,0:T(8,128)(2,1)S(1)}, u32[]{:S(2)}, u32[]{:S(2)}) async-start(bf16[16,4,80,128]{3,2,1,0:T(8,128)(2,1)} %copy-done.3), calls=%async_computation.2 | async-start | bytes 2621440 | tf_op jit(solution)/shard_map/all_to_all | solution.py:485
  168.4 22.2 %collective-permute-start.17 = (bf16[128,1024]{1,0:T(8,128)(2,1)}, bf16[128,1024]{1,0:T(8,128)(2,1)}, u32[]{:S(2)}, u32[]{:S(2)}) collective-permute-start(bf16[128,1024]{1,0:T(8,128)(2,1)} %get-tuple-element.62), channel_id=1, source_target_pairs={{0,2},{1,3},{2,0},{3,1},{4,6},{5,7},{6,4},{7,5},{8,10},{9,11},{10,... | collective-permute-start | bytes 786440 | tf_op jit(solution)/shard_map/ppermute | solution.py:452
  168.5 23.4 %collective-permute-start.18 = (bf16[128,1024]{1,0:T(8,128)(2,1)}, bf16[128,1024]{1,0:T(8,128)(2,1)}, u32[]{:S(2)}, u32[]{:S(2)}) collective-permute-start(bf16[128,1024]{1,0:T(8,128)(2,1)} %get-tuple-element.63), channel_id=1, source_target_pairs={{0,4},{1,5},{2,6},{3,7},{4,0},{5,1},{6,2},{7,3},{8,12},{9,13},{10,... | collective-permute-start | bytes 786440 | tf_op jit(solution)/shard_map/ppermute | solution.py:452
  171.2 25.4 %copy-start.7 = (bf16[128,1024]{1,0:T(8,128)(2,1)S(1)}, bf16[128,1024]{1,0:T(8,128)(2,1)}, u32[]{:S(2)}) copy-start(bf16[128,1024]{1,0:T(8,128)(2,1)} %copy-done.6) | copy-start | bytes 786436
  171.2 25.5 %copy-start.9 = (bf16[128,1024]{1,0:T(8,128)(2,1)S(1)}, bf16[128,1024]{1,0:T(8,128)(2,1)}, u32[]{:S(2)}) copy-start(bf16[128,1024]{1,0:T(8,128)(2,1)} %copy-done.8) | copy-start | bytes 786436
  171.2 25.5 %copy-start.11 = (bf16[128,1024]{1,0:T(8,128)(2,1)S(1)}, bf16[128,1024]{1,0:T(8,128)(2,1)}, u32[]{:S(2)}) copy-start(bf16[128,1024]{1,0:T(8,128)(2,1)} %copy-done.10) | copy-start | bytes 786436
  171.2 25.5 %copy-start.27 = (s32[4]{0:T(128)S(1)}, s32[4]{0:T(128)}, u32[]{:S(2)}) copy-start(s32[4]{0:T(128)} %copy-done.26) | copy-start | bytes 52
  171.2 20.7 %collective-permute-start.19 = (bf16[128,1024]{1,0:T(8,128)(2,1)}, bf16[128,1024]{1,0:T(8,128)(2,1)}, u32[]{:S(2)}, u32[]{:S(2)}) collective-permute-start(bf16[128,1024]{1,0:T(8,128)(2,1)} %get-tuple-element.64), channel_id=1, source_target_pairs={{0,6},{1,7},{2,4},{3,5},{4,2},{5,3},{6,0},{7,1},{8,14},{9,15},{10,... | collective-permute-start | bytes 786440 | tf_op jit(solution)/shard_map/ppermute | solution.py:452
  175.9 14.7 %copy-start.37 = (bf16[8,80,128]{2,1,0:T(8,128)(2,1)S(1)}, bf16[8,80,128]{2,1,0:T(8,128)(2,1)}, u32[]{:S(2)}) copy-start(bf16[8,80,128]{2,1,0:T(8,128)(2,1)} %copy-done.36) | copy-start | bytes 491524
  175.9 19.5 %collective-permute-start.25 = (bf16[8,80,128]{2,1,0:T(8,128)(2,1)}, bf16[8,80,128]{2,1,0:T(8,128)(2,1)S(1)}, u32[]{:S(2)}, u32[]{:S(2)}) collective-permute-start(bf16[8,80,128]{2,1,0:T(8,128)(2,1)} %get-tuple-element.74), channel_id=1, source_target_pairs={{0,2},{1,3},{2,0},{3,1},{4,6},{5,7},{6,4},{7,5},{8,10},{9,11},{10,... | collective-permute-start | bytes 491528 | tf_op jit(solution)/shard_map/ppermute | solution.py:452
  175.9 26.0 %collective-permute-start.26 = (bf16[8,80,128]{2,1,0:T(8,128)(2,1)}, bf16[8,80,128]{2,1,0:T(8,128)(2,1)S(1)}, u32[]{:S(2)}, u32[]{:S(2)}) collective-permute-start(bf16[8,80,128]{2,1,0:T(8,128)(2,1)} %get-tuple-element.75), channel_id=1, source_target_pairs={{0,4},{1,5},{2,6},{3,7},{4,0},{5,1},{6,2},{7,3},{8,12},{9,13},{10,... | collective-permute-start | bytes 491528 | tf_op jit(solution)/shard_map/ppermute | solution.py:452
  190.0 9.2 %copy-start.20 = (bf16[128,1024]{1,0:T(8,128)(2,1)S(1)}, bf16[128,1024]{1,0:T(8,128)(2,1)}, u32[]{:S(2)}) copy-start(bf16[128,1024]{1,0:T(8,128)(2,1)} %get-tuple-element.61.rest_0_) | copy-start | bytes 786436
  190.6 11.3 %collective-permute-start.27 = (bf16[8,80,128]{2,1,0:T(8,128)(2,1)S(1)}, bf16[8,80,128]{2,1,0:T(8,128)(2,1)S(1)}, u32[]{:S(2)}, u32[]{:S(2)}) collective-permute-start(bf16[8,80,128]{2,1,0:T(8,128)(2,1)S(1)} %copy-done.37), channel_id=1, source_target_pairs={{0,6},{1,7},{2,4},{3,5},{4,2},{5,3},{6,0},{7,1},{8,14},{9,15},{10,... | collective-permute-start | bytes 491528 | tf_op jit(solution)/shard_map/ppermute | solution.py:452
  192.0 10.0 %collective-permute-start.21 = (bf16[8,80,128]{2,1,0:T(8,128)(2,1)S(1)}, bf16[8,80,128]{2,1,0:T(8,128)(2,1)S(1)}, u32[]{:S(2)}, u32[]{:S(2)}) collective-permute-start(bf16[8,80,128]{2,1,0:T(8,128)(2,1)S(1)} %get-tuple-element.68), channel_id=1, source_target_pairs={{0,2},{1,3},{2,0},{3,1},{4,6},{5,7},{6,4},{7,5},{8,10},{9,11},{10,... | collective-permute-start | bytes 491528 | tf_op jit(solution)/shard_map/ppermute | solution.py:452
  192.0 10.0 %collective-permute-start.22 = (bf16[8,80,128]{2,1,0:T(8,128)(2,1)S(1)}, bf16[8,80,128]{2,1,0:T(8,128)(2,1)S(1)}, u32[]{:S(2)}, u32[]{:S(2)}) collective-permute-start(bf16[8,80,128]{2,1,0:T(8,128)(2,1)S(1)} %get-tuple-element.69), channel_id=1, source_target_pairs={{0,4},{1,5},{2,6},{3,7},{4,0},{5,1},{6,2},{7,3},{8,12},{9,13},{10,... | collective-permute-start | bytes 491528 | tf_op jit(solution)/shard_map/ppermute | solution.py:452
  195.4 8.8 %collective-permute-start.23 = (bf16[8,80,128]{2,1,0:T(8,128)(2,1)S(1)}, bf16[8,80,128]{2,1,0:T(8,128)(2,1)S(1)}, u32[]{:S(2)}, u32[]{:S(2)}) collective-permute-start(bf16[8,80,128]{2,1,0:T(8,128)(2,1)S(1)} %get-tuple-element.70), channel_id=1, source_target_pairs={{0,6},{1,7},{2,4},{3,5},{4,2},{5,3},{6,0},{7,1},{8,14},{9,15},{10,... | collective-permute-start | bytes 491528 | tf_op jit(solution)/shard_map/ppermute | solution.py:452
  199.2 5.0 %copy-start.24 = (bf16[8,80,128]{2,1,0:T(8,128)(2,1)S(1)}, bf16[8,80,128]{2,1,0:T(8,128)(2,1)}, u32[]{:S(2)}) copy-start(bf16[8,80,128]{2,1,0:T(8,128)(2,1)} %copy-done.23) | copy-start | bytes 491524
  (26 other events, 29.3 us)
